TPU v7x, 256 devices: a whole 4x4x8 slice. The times are simulated.
256 devices in a mesh: grp: 4 (over x_lo, core), pts: 64 (over y, x_hi, z).
Axes of the slice: x: 4 (x_hi: 2, x_lo: 2; x = x_hi * 2 + x_lo), y: 4, z: 8, core: 2. Of those that a mesh axis runs over, the one named last changes fastest.
Arguments:
- points: float32 [65536, 2048], P(('grp', 'pts')), may hold values from -2 to 2
- log_factor: float32 [65536, 256], P(('grp', 'pts')), may hold values from -40 to 320
- masses: float32 [65536], P(('grp', 'pts')), may hold values from 0.1 to 12
Outputs:
- factors: float32 [65536, 256], P(('grp', 'pts'))
All inputs are finite; a program needn't handle non-finite values. Where the computation divides by a largest or mean magnitude, that divisor is 1e-20 or more.
Results may differ from a plain program's by a relative error of at most 0.0003.
Values sent between devices are 32-bit elements; how exact they have to be, the bound alone decides.
A program may use at most 64 MiB of HBM per device.

v0:
```python
import functools

import jax
import jax.numpy as jnp
from jax import lax
from jax.sharding import Mesh
from jax.sharding import PartitionSpec as P

ITERS = 2
GRP = ("grp_0", "grp_1")
PTS = ("pts_0", "pts_1", "pts_2")
GRP_PTS = ("grp_0", "grp_1", "pts_0", "pts_1", "pts_2")


step_scale = 4.0
highest = lax.Precision.HIGHEST


def in_blocks(x, dim, length):
    lengths = x.shape
    tiles = x.reshape(*lengths[:dim], length, lengths[dim] // length, *lengths[dim + 1 :])
    return jnp.moveaxis(tiles, dim, 0)


def summed_on_arrival(x, axis, dim):
    length = lax.axis_size(axis)
    tiles = lax.all_to_all(in_blocks(x, dim, length), axis, 0, 0, tiled=True)
    return jnp.sum(tiles, axis=0)


def copy_for_each(x, axis):
    copies = jnp.broadcast_to(x, (lax.axis_size(axis), *x.shape))
    return lax.all_to_all(copies, axis, split_axis=0, concat_axis=0, tiled=True)


def taken_together(x, axis):
    return copy_for_each(x, axis).sum(axis=0)


def in_one_piece(arrays, axis, dim, along):
    widths = [a.shape[along] for a in arrays]
    both = jnp.concatenate(arrays, axis=along)
    out = lax.all_gather(both, axis, axis=dim, tiled=True)
    return tuple(jnp.split(out, [sum(widths[:k]) for k in range(1, len(widths))], axis=along))


def in_order(tiles, dim):
    lengths = list(tiles.shape[1:])
    lengths[dim] *= tiles.shape[0]
    return jnp.moveaxis(tiles, 0, dim).reshape(lengths)


def all_blocks(x, axes, sequence):
    tiles = x
    for k in sequence:
        tiles = lax.all_gather(tiles, axes[k])
    done = sequence[::-1]
    back = [done.index(k) for k in range(len(axes))]
    tiles = tiles.transpose(*back, *range(len(axes), tiles.ndim))
    return tiles.reshape(-1, *x.shape)


def gather_axes(x, axes, sequence, dim):
    return in_order(all_blocks(x, axes, sequence), dim)


def by_axis(x, axes):
    return functools.reduce(lax.pmax, axes, x)


def contract_rows(left_block, right_block):
    return lax.dot_general(
        left_block,
        right_block,
        (((0,), (0,)), ((), ())),
        precision=highest,
        preferred_element_type=jnp.float32,
    )


def split_sides(gathered):
    source_total = gathered[0] + gathered[1] + gathered[2]
    return (source_total, gathered[3])


def body(points, log_factor, masses):
    target = lax.axis_index(GRP) == 3
    squares = jnp.sum(points * points, axis=1)
    rank_width = log_factor.shape[1]
    for iteration in range(ITERS):
        weights = jax.nn.softmax(log_factor, axis=1)
        scaled = weights * masses[:, None]
        column_sums = jnp.sum(scaled, axis=0)
        norm_moment = jnp.dot(
            squares, scaled, precision=highest, preferred_element_type=jnp.float32
        )
        statistics = jnp.stack([norm_moment, column_sums])
        moment_shard = summed_on_arrival(contract_rows(points, scaled), PTS, 0)
        side_statistics = taken_together(statistics, PTS)
        gathered_shards, gathered_statistics = in_one_piece(
            (moment_shard[None], side_statistics[None]), GRP, 0, 1
        )
        source_shard, target_shard = split_sides(gathered_shards)
        facing_shard = jnp.where(target, source_shard, target_shard)
        cross_term = jnp.dot(
            points,
            gather_axes(facing_shard, PTS, (1, 2, 0), 0),
            precision=highest,
            preferred_element_type=jnp.float32,
        )
        source_statistics, target_statistics = split_sides(gathered_statistics)
        source_columns = source_statistics[1]
        target_columns = target_statistics[1]
        source_mass = jnp.sum(source_columns)
        target_mass = jnp.sum(target_columns)
        marginal = 0.5 * (source_columns / source_mass + target_columns / target_mass)
        facing_mass = jnp.where(target, source_mass, target_mass)
        facing_columns = jnp.where(target, source_columns, target_columns)
        facing_norms = jnp.where(target, source_statistics[0], target_statistics[0])
        gradient = (
            squares[:, None] * (facing_columns / facing_mass)[None, :]
            - 2.0 * (cross_term / facing_mass)
            + (facing_norms / facing_mass)[None, :]
        ) / marginal[None, :]
        centred = gradient - jnp.mean(gradient, axis=1, keepdims=True)
        largest = by_axis(jnp.max(jnp.abs(centred)), GRP_PTS)
        log_factor = log_factor - step_scale / (largest + 1e-06) * gradient
    return rank_width * jax.nn.softmax(log_factor, axis=1)


def solution(mesh):
    split = Mesh(mesh.devices.reshape(2, 2, 4, 2, 8), ("grp_0", "grp_1", "pts_0", "pts_1", "pts_2"))
    return jax.shard_map(
        body,
        mesh=split,
        in_specs=(P(GRP_PTS, None), P(GRP_PTS, None), P(GRP_PTS)),
        out_specs=P(GRP_PTS, None),
        check_vma=False,
    )
```

profile of v0, /device:TPU:1, one launch (start us, length us, event | category | flops | bytes accessed | tf_op | source)
XLA Modules:
  0.0 411.8 jit_solution(13241688246355370390)
XLA Ops:
  11.9 15.1 %all-to-all-start.1 = ((f32[64,2,256]{2,1,0:T(2,128)}), f32[64,2,256]{2,1,0:T(2,128)S(1)}, u32[]{:S(2)}, u32[]{:S(2)}) async-start(f32[64,2,256]{2,1,0:T(2,128)} %broadcast_in_dim.13), calls=%async_computation.1 | async-start | bytes 262144 | tf_op jit(solution)/shard_map/all_to_all | solution.py:33
  33.2 5.3 %all-to-all-done.1 = f32[64,2,256]{2,1,0:T(2,128)S(1)} async-done(((f32[64,2,256]{2,1,0:T(2,128)}), f32[64,2,256]{2,1,0:T(2,128)S(1)}, u32[]{:S(2)}, u32[]{:S(2)}) %all-to-all-start.1) | async-done | bytes 131104 | tf_op jit(solution)/shard_map/all_to_all | solution.py:33
  38.5 7.1 %all-to-all-start = ((f32[64,32,256]{2,1,0:T(8,128)}), f32[64,32,256]{2,1,0:T(8,128)}, u32[]{:S(2)}, u32[]{:S(2)}) async-start(f32[64,32,256]{2,1,0:T(8,128)} %bitcast.56), calls=%async_computation | async-start | bytes 4194304 | tf_op jit(solution)/shard_map/all_to_all | solution.py:27
  45.8 48.1 %all-to-all-done = f32[64,32,256]{2,1,0:T(8,128)} async-done(((f32[64,32,256]{2,1,0:T(8,128)}), f32[64,32,256]{2,1,0:T(8,128)}, u32[]{:S(2)}, u32[]{:S(2)}) %all-to-all-start) | async-done | bytes 2097184 | tf_op jit(solution)/shard_map/all_to_all | solution.py:27
  95.7 10.3 %all_gather.38 = f32[4,34,256]{2,1,0:T(8,128)S(1)} all-gather(f32[1,34,256]{2,1,0:T(8,128)S(1)} %pad_maximum_fusion), channel_id=1, replica_groups=mesh['grp_0'=2,'grp_1'=2,'pts_0'=4,'pts_1'=2,'pts_2'=8] {'grp_0','grp_1'}, dimensions={0}, use_global_device_ids=true | all-gather | bytes 174080 | tf_op jit(solution)/shard_map/all_gather | solution.py:43
  106.1 4.9 %all_gather.39 = f32[2,32,256]{2,1,0:T(8,128)S(1)} all-gather(f32[1,32,256]{2,1,0:T(8,128)S(1)} %slice_select_fusion.1), channel_id=1, replica_groups=mesh['grp_0'=2,'grp_1'=2,'pts_0'=4,'pts_1'=2,'pts_2'=8] {'pts_1'}, dimensions={0}, use_global_device_ids=true | all-gather | bytes 98304 | tf_op jit(solution)/shard_map/all_gather | solution.py:56
  111.0 21.7 %all-gather = f32[16,32,256]{2,1,0:T(8,128)} all-gather(f32[2,32,256]{2,1,0:T(8,128)S(1)} %all_gather.39), channel_id=2, replica_groups=mesh['grp_0'=2,'grp_1'=2,'pts_0'=4,'pts_1'=2,'pts_2'=8] {'pts_2'}, dimensions={0}, use_global_device_ids=true | all-gather | bytes 589824 | tf_op jit(solution)/shard_map/all_gather | solution.py:56
  135.9 31.7 %all-gather.7.cloned.1.call-done = f32[32,2,32,256]{3,2,1,0:T(8,128)} async-done(((f32[8,2,32,256]{3,2,1,0:T(8,128)}), f32[32,2,32,256]{3,2,1,0:T(8,128)}) %all-gather.7.cloned.1.call-update) | async-done | bytes 2097168 | tf_op jit(solution)/shard_map/all_gather | solution.py:56
  178.1 4.6 %pmax.71 = f32[]{:T(128)} all-reduce(f32[]{:T(128)} %pmax.70), channel_id=1, replica_groups=mesh['grp_0'=2,'grp_1'=2,'pts_0'=4,'pts_1'=2,'pts_2'=8] {'grp_1'}, use_global_device_ids=true, to_apply=%region_11.12 | all-reduce | flops 1 | bytes 8 | tf_op jit(solution)/shard_map/pmax | solution.py:68
  182.6 7.1 %pmax.72 = f32[]{:T(128)} all-reduce(f32[]{:T(128)} %pmax.71), channel_id=1, replica_groups=mesh['grp_0'=2,'grp_1'=2,'pts_0'=4,'pts_1'=2,'pts_2'=8] {'pts_0'}, use_global_device_ids=true, to_apply=%region_12.13 | all-reduce | flops 1 | bytes 8 | tf_op jit(solution)/shard_map/pmax | solution.py:68
  189.8 5.9 %pmax.73 = f32[]{:T(128)} all-reduce(f32[]{:T(128)} %pmax.72), channel_id=1, replica_groups=mesh['grp_0'=2,'grp_1'=2,'pts_0'=4,'pts_1'=2,'pts_2'=8] {'pts_1'}, use_global_device_ids=true, to_apply=%region_13.14 | all-reduce | flops 1 | bytes 8 | tf_op jit(solution)/shard_map/pmax | solution.py:68
  195.7 14.3 %pmax.74 = f32[]{:T(128)} all-reduce(f32[]{:T(128)} %pmax.73), channel_id=1, replica_groups=mesh['grp_0'=2,'grp_1'=2,'pts_0'=4,'pts_1'=2,'pts_2'=8] {'pts_2'}, use_global_device_ids=true, to_apply=%region_14.15 | all-reduce | flops 1 | bytes 8 | tf_op jit(solution)/shard_map/pmax | solution.py:68
  212.0 8.4 %all-to-all-start.3 = ((f32[64,2,256]{2,1,0:T(2,128)}), f32[64,2,256]{2,1,0:T(2,128)S(1)}, u32[]{:S(2)}, u32[]{:S(2)}) async-start(f32[64,2,256]{2,1,0:T(2,128)} %broadcast_in_dim.16), calls=%async_computation.3 | async-start | bytes 262144 | tf_op jit(solution)/shard_map/all_to_all | solution.py:33
  226.6 5.1 %all-to-all-done.3 = f32[64,2,256]{2,1,0:T(2,128)S(1)} async-done(((f32[64,2,256]{2,1,0:T(2,128)}), f32[64,2,256]{2,1,0:T(2,128)S(1)}, u32[]{:S(2)}, u32[]{:S(2)}) %all-to-all-start.3) | async-done | bytes 131104 | tf_op jit(solution)/shard_map/all_to_all | solution.py:33
  231.8 7.1 %all-to-all-start.2 = ((f32[64,32,256]{2,1,0:T(8,128)}), f32[64,32,256]{2,1,0:T(8,128)}, u32[]{:S(2)}, u32[]{:S(2)}) async-start(f32[64,32,256]{2,1,0:T(8,128)} %bitcast.57), calls=%async_computation.2 | async-start | bytes 4194304 | tf_op jit(solution)/shard_map/all_to_all | solution.py:27
  239.1 41.8 %all-to-all-done.2 = f32[64,32,256]{2,1,0:T(8,128)} async-done(((f32[64,32,256]{2,1,0:T(8,128)}), f32[64,32,256]{2,1,0:T(8,128)}, u32[]{:S(2)}, u32[]{:S(2)}) %all-to-all-start.2) | async-done | bytes 2097184 | tf_op jit(solution)/shard_map/all_to_all | solution.py:27
  282.6 16.4 %all_gather.44 = f32[4,34,256]{2,1,0:T(8,128)S(1)} all-gather(f32[1,34,256]{2,1,0:T(8,128)S(1)} %pad_maximum_fusion.1), channel_id=1, replica_groups=mesh['grp_0'=2,'grp_1'=2,'pts_0'=4,'pts_1'=2,'pts_2'=8] {'grp_0','grp_1'}, dimensions={0}, use_global_device_ids=true | all-gather | bytes 174080 | tf_op jit(solution)/shard_map/all_gather | solution.py:43
  299.1 4.9 %all_gather.45 = f32[2,32,256]{2,1,0:T(8,128)S(1)} all-gather(f32[1,32,256]{2,1,0:T(8,128)S(1)} %slice_select_fusion), channel_id=1, replica_groups=mesh['grp_0'=2,'grp_1'=2,'pts_0'=4,'pts_1'=2,'pts_2'=8] {'pts_1'}, dimensions={0}, use_global_device_ids=true | all-gather | bytes 98304 | tf_op jit(solution)/shard_map/all_gather | solution.py:56
  304.0 21.3 %all-gather.2 = f32[16,32,256]{2,1,0:T(8,128)} all-gather(f32[2,32,256]{2,1,0:T(8,128)S(1)} %all_gather.45), channel_id=4, replica_groups=mesh['grp_0'=2,'grp_1'=2,'pts_0'=4,'pts_1'=2,'pts_2'=8] {'pts_2'}, dimensions={0}, use_global_device_ids=true | all-gather | bytes 589824 | tf_op jit(solution)/shard_map/all_gather | solution.py:56
  329.1 31.7 %all-gather.9.cloned.1.call-done = f32[32,2,32,256]{3,2,1,0:T(8,128)} async-done(((f32[8,2,32,256]{3,2,1,0:T(8,128)}), f32[32,2,32,256]{3,2,1,0:T(8,128)}) %all-gather.9.cloned.1.call-update) | async-done | bytes 2097168 | tf_op jit(solution)/shard_map/all_gather | solution.py:56
  371.3 4.6 %pmax.76 = f32[]{:T(128)} all-reduce(f32[]{:T(128)} %pmax.75), channel_id=1, replica_groups=mesh['grp_0'=2,'grp_1'=2,'pts_0'=4,'pts_1'=2,'pts_2'=8] {'grp_1'}, use_global_device_ids=true, to_apply=%region_25.26 | all-reduce | flops 1 | bytes 8 | tf_op jit(solution)/shard_map/pmax | solution.py:68
  375.8 7.1 %pmax.77 = f32[]{:T(128)} all-reduce(f32[]{:T(128)} %pmax.76), channel_id=1, replica_groups=mesh['grp_0'=2,'grp_1'=2,'pts_0'=4,'pts_1'=2,'pts_2'=8] {'pts_0'}, use_global_device_ids=true, to_apply=%region_26.27 | all-reduce | flops 1 | bytes 8 | tf_op jit(solution)/shard_map/pmax | solution.py:68
  383.0 5.9 %pmax.78 = f32[]{:T(128)} all-reduce(f32[]{:T(128)} %pmax.77), channel_id=1, replica_groups=mesh['grp_0'=2,'grp_1'=2,'pts_0'=4,'pts_1'=2,'pts_2'=8] {'pts_1'}, use_global_device_ids=true, to_apply=%region_27.28 | all-reduce | flops 1 | bytes 8 | tf_op jit(solution)/shard_map/pmax | solution.py:68
  388.9 14.3 %pmax.79 = f32[]{:T(128)} all-reduce(f32[]{:T(128)} %pmax.78), channel_id=1, replica_groups=mesh['grp_0'=2,'grp_1'=2,'pts_0'=4,'pts_1'=2,'pts_2'=8] {'pts_2'}, use_global_device_ids=true, to_apply=%region_28.29 | all-reduce | flops 1 | bytes 8 | tf_op jit(solution)/shard_map/pmax | solution.py:68
  (55 shorter events, 49.0 us)
Async XLA Ops:
  6.5 4.2 %copy-start.1 = (f32[256]{0:T(256)S(1)}, f32[256]{0:T(256)}, u32[]{:S(2)}) copy-start(f32[256]{0:T(256)} %param.5) | copy-start | bytes 3076
  8.7 18.4 %copy-start = (f32[256,2048]{1,0:T(8,128)S(1)}, f32[256,2048]{1,0:T(8,128)}, u32[]{:S(2)}) copy-start(f32[256,2048]{1,0:T(8,128)} %param.3) | copy-start | bytes 6291460
  11.9 26.6 %all-to-all-start.1 = ((f32[64,2,256]{2,1,0:T(2,128)}), f32[64,2,256]{2,1,0:T(2,128)S(1)}, u32[]{:S(2)}, u32[]{:S(2)}) async-start(f32[64,2,256]{2,1,0:T(2,128)} %broadcast_in_dim.13), calls=%async_computation.1 | async-start | bytes 262144 | tf_op jit(solution)/shard_map/all_to_all | solution.py:33
  38.5 55.4 %all-to-all-start = ((f32[64,32,256]{2,1,0:T(8,128)}), f32[64,32,256]{2,1,0:T(8,128)}, u32[]{:S(2)}, u32[]{:S(2)}) async-start(f32[64,32,256]{2,1,0:T(8,128)} %bitcast.56), calls=%async_computation | async-start | bytes 4194304 | tf_op jit(solution)/shard_map/all_to_all | solution.py:27
  45.7 121.9 %all-gather.7.cloned.1.call-start = ((), (), s32[]{:S(2)}) async-start(), calls=%async_computation.4 | async-start | bytes 2621440 | tf_op jit(solution)/shard_map/all_gather | solution.py:56
  212.0 19.8 %all-to-all-start.3 = ((f32[64,2,256]{2,1,0:T(2,128)}), f32[64,2,256]{2,1,0:T(2,128)S(1)}, u32[]{:S(2)}, u32[]{:S(2)}) async-start(f32[64,2,256]{2,1,0:T(2,128)} %broadcast_in_dim.16), calls=%async_computation.3 | async-start | bytes 262144 | tf_op jit(solution)/shard_map/all_to_all | solution.py:33
  231.8 49.1 %all-to-all-start.2 = ((f32[64,32,256]{2,1,0:T(8,128)}), f32[64,32,256]{2,1,0:T(8,128)}, u32[]{:S(2)}, u32[]{:S(2)}) async-start(f32[64,32,256]{2,1,0:T(8,128)} %bitcast.57), calls=%async_computation.2 | async-start | bytes 4194304 | tf_op jit(solution)/shard_map/all_to_all | solution.py:27
  238.9 121.9 %all-gather.9.cloned.1.call-start = ((), (), s32[]{:S(2)}) async-start(), calls=%async_computation.5 | async-start | bytes 2621440 | tf_op jit(solution)/shard_map/all_gather | solution.py:56
Sparse Core Ops, SparseCore 0:
  132.9 34.6 all-gather.6
  325.5 35.3 all-gather.8
where the time goes:
time: 419 us; the launch traced here: 412 us
  waiting for transfers between devices  164 us (39%)
  blocking collectives  152 us (36%)
  starting transfers between devices  37.9 us (9%)
  between operations  17.5 us (4%)
  matrix products  14.3 us (3%)
  other arithmetic  13.1 us (3%)
  local copies, waits for them, and re-layouts  12.7 us (3%)
    all_to_all x2, waiting for transfers between devices, summed_on_arrival(): tiles = lax.all_to_all(in_blocks(x, dim, length), axis, 0, 0, tiled=True)  90 us
    pmax x10, blocking collectives, by_axis(): return functools.reduce(lax.pmax, axes, x)  72.7 us
    all_gather x2, waiting for transfers between devices, all_blocks(): tiles = lax.all_gather(tiles, axes[k])  63.4 us
    all_gather x4, blocking collectives, all_blocks(): tiles = lax.all_gather(tiles, axes[k])  52.9 us
    all_gather x2, blocking collectives, in_one_piece(): out = lax.all_gather(both, axis, axis=dim, tiled=True)  26.8 us
    all_to_all x2, starting transfers between devices, copy_for_each(): return lax.all_to_all(copies, axis, split_axis=0, concat_axis=0, tiled=True)  23.6 us
    all_to_all x2, starting transfers between devices, summed_on_arrival(): tiles = lax.all_to_all(in_blocks(x, dim, length), axis, 0, 0, tiled=True)  14.3 us
    all_to_all x2, waiting for transfers between devices, copy_for_each(): return lax.all_to_all(copies, axis, split_axis=0, concat_axis=0, tiled=True)  10.5 us
  transfers between devices with their start and end apart: 6, of which 6 were waited for; matrix products, arithmetic and copies ran while one was open for 4% of the time, Pallas kernels for 0%

commit v1 on v0

v1 whole, which is shorter than its diff:
```python
import functools

import jax
import jax.numpy as jnp
from jax import lax
from jax.experimental import pallas as pl
from jax.experimental.pallas import tpu as pltpu
from jax.sharding import Mesh
from jax.sharding import PartitionSpec as P

ITERS = 2
STEP_SCALE = 4.0
AXES = ("xl", "c", "y", "xh", "z")
NY, NZ, NX = 4, 8, 4
ROWS = 256
RANK = 256
HALF = 1024
YB = HALF // NY
ZB = YB // NZ
ZS = ZB + 8
HIGHEST = lax.Precision.HIGHEST


def dot0(a, b):
    return lax.dot_general(
        a, b, (((0,), (0,)), ((), ())), precision=HIGHEST, preferred_element_type=jnp.float32
    )


def dot1(a, b):
    return lax.dot_general(
        a, b, (((1,), (0,)), ((), ())), precision=HIGHEST, preferred_element_type=jnp.float32
    )


def kernel(
    points, lf_in, mass, out,
    pts, lf, meta, meta_out, scaled, mom, ring1, ring2, stat, zsend, zrecv, xall, gath, acc, part,
    mx, grad, fin,
    s_pts, r_pts, s_lf, r_lf, s_meta, r_meta, s_sc, r_sc, s_r1, r_r1, s_r2, r_r2, s_st, r_st,
    s_z, r_z, s_x, r_x, s_gz, r_gz, s_gy, r_gy, s_pt, r_pt, s_mc, r_mc, s_my, r_my, s_mz, r_mz,
    s_fin, r_fin,
):
    xl, c, y, xh, z = (lax.axis_index(a) for a in AXES)
    x = 2 * xh + xl
    other = 1 - c
    swp = xl * ((c + xh) % 2)
    vc = (c + swp) % 2
    vxh = (xh + swp) % 2
    swapped = swp == 1

    def at(c_=None, x_=None, y_=None, z_=None):
        x_ = x if x_ is None else x_
        return (
            x_ % 2,
            c if c_ is None else c_,
            y if y_ is None else y_,
            x_ // 2,
            z if z_ is None else z_,
        )

    xq = 2 * vxh + xl
    yo = [(y + j) % NY for j in range(NY)]
    zo = [(z + j) % NZ for j in range(NZ)]
    xo = [(x + j) % NX for j in range(NX)]
    cx = [(c if i == 0 else other, xo[j]) for i in range(2) for j in range(NX)]

    def rdma(src, dst, ss, rs, dev):
        return pltpu.make_async_remote_copy(
            src_ref=src, dst_ref=dst, send_sem=ss, recv_sem=rs, device_id=dev,
            device_id_type=pl.DeviceIdType.MESH,
        )

    barrier = pltpu.get_barrier_semaphore()
    peers = [at(c_=a, x_=b) for a, b in cx[1:]]
    peers += [at(y_=b) for b in yo[1:]] + [at(z_=b) for b in zo[1:]]
    for p in peers:
        pl.semaphore_signal(barrier, inc=1, device_id=p, device_id_type=pl.DeviceIdType.MESH)
    pl.semaphore_wait(barrier, len(peers))

    def cols(h, b):
        return points.at[:, pl.ds(pl.multiple_of(h * HALF + b * YB, YB), YB)]

    order = [yo[2], yo[1], yo[3], yo[0]]
    mine = pl.ds(pl.multiple_of(vc * ROWS, ROWS), ROWS)

    def half_out(b):
        return rdma(cols(other, b), pts.at[b, mine], s_pts.at[0, b], r_pts.at[b, vc],
                    at(c_=other, x_=xq))

    def half_own(b):
        return rdma(cols(c, b), pts.at[b, mine], s_pts.at[1, b], r_pts.at[b, vc],
                    at(c_=c, x_=xq))

    def half_local(b):
        return pltpu.make_async_copy(cols(c, b), pts.at[b, mine], r_pts.at[b, vc])

    lf_remote = rdma(lf_in, lf, s_lf, r_lf, at(c_=vc, x_=xq))
    lf_local = pltpu.make_async_copy(lf_in, lf, r_lf)

    @pl.when(swapped)
    def _():
        lf_remote.start()
        for b in order:
            half_out(b).start()
            half_own(b).start()

    @pl.when(jnp.logical_not(swapped))
    def _():
        lf_local.start()
        for b in order:
            half_out(b).start()
            half_local(b).start()

    squares = jnp.zeros((ROWS, 1), jnp.float32)
    for k in range(8):
        part_k = points[:, k * 256 : (k + 1) * 256]
        squares += jnp.sum(part_k * part_k, axis=1, keepdims=True)
    lane = lax.broadcasted_iota(jnp.int32, (ROWS, 128), 1)
    meta_out[...] = jnp.where(
        lane == 0, squares, jnp.where(lane == 1, 1.0, jnp.where(lane == 2, mass[...], 0.0))
    )
    meta_remote = rdma(meta_out, meta.at[mine], s_meta.at[0], r_meta.at[vc],
                       at(c_=other, x_=xq))
    meta_own = rdma(meta_out, meta.at[mine], s_meta.at[1], r_meta.at[vc], at(c_=c, x_=xq))
    meta_local = pltpu.make_async_copy(meta_out, meta.at[mine], r_meta.at[vc])
    meta_remote.start()

    @pl.when(swapped)
    def _():
        meta_own.start()

    @pl.when(jnp.logical_not(swapped))
    def _():
        meta_local.start()

    own = pl.ds(pl.multiple_of(c * ROWS, ROWS), ROWS)
    oth = pl.ds(pl.multiple_of(other * ROWS, ROWS), ROWS)
    lf_remote.wait_recv()
    for v in range(2):
        rdma(meta_out, meta.at[pl.ds(v * ROWS, ROWS)], s_meta.at[0], r_meta.at[v],
             at(c_=other)).wait_recv()

    def wait_points(b):
        for v in range(2):
            rdma(cols(c, b), pts.at[b, pl.ds(v * ROWS, ROWS)], s_pts.at[0, b], r_pts.at[b, v],
                 at(c_=other)).wait_recv()

    def step(it, _):
        v = lf[...]
        e = jnp.exp(v - jnp.max(v, axis=1, keepdims=True))
        mass_own = meta[own, 2:3]
        scaled[it, own] = e / jnp.sum(e, axis=1, keepdims=True) * mass_own
        cp = rdma(scaled.at[it, own], scaled.at[it, own], s_sc.at[it], r_sc.at[it], at(c_=other))
        cp.start()
        cp.wait_send()
        rdma(scaled.at[it, oth], scaled.at[it, oth], s_sc.at[it], r_sc.at[it],
             at(c_=other)).wait_recv()

        stat[it, 0] = dot0(meta[...], scaled[it])[:8]
        st = [rdma(stat.at[it, 0], stat.at[it, j], s_st.at[it, j], r_st.at[it, j], at(y_=yo[j]))
              for j in range(1, NY)]
        for cpy in st:
            cpy.start()

        def moment(b):
            @pl.when(it == 0)
            def _():
                wait_points(b)
            return dot0(pts[b], scaled[it])

        mom[it, 2] = moment(yo[2])
        up1 = rdma(mom.at[it, 2, pl.ds(0, 128)], ring1.at[it, 0], s_r1.at[it, 0],
                   r_r1.at[it, 0], at(y_=yo[1]))
        dn1 = rdma(mom.at[it, 2, pl.ds(128, 128)], ring1.at[it, 1], s_r1.at[it, 1],
                   r_r1.at[it, 1], at(y_=yo[3]))
        up1.start()
        dn1.start()
        m1 = moment(yo[1])
        up1.wait_recv()
        mom[it, 1, :128] = m1[:128] + ring1[it, 0]
        mom[it, 1, 128:] = m1[128:]
        up2 = rdma(mom.at[it, 1], ring2.at[it, 0], s_r2.at[it, 0], r_r2.at[it, 0], at(y_=yo[1]))
        up2.start()
        m3 = moment(yo[3])
        dn1.wait_recv()
        mom[it, 3, :128] = m3[:128]
        mom[it, 3, 128:] = m3[128:] + ring1[it, 1]
        dn2 = rdma(mom.at[it, 3], ring2.at[it, 1], s_r2.at[it, 1], r_r2.at[it, 1], at(y_=yo[3]))
        dn2.start()
        mom[it, 0] = moment(yo[0])
        for cpy in st:
            cpy.wait_recv()
        stats_y = stat[it, 0] + stat[it, 1] + stat[it, 2] + stat[it, 3]
        for k in range(NZ):
            zsend[it, k, ZB:] = stats_y
        up2.wait_recv()
        dn2.wait_recv()
        for k in range(NZ):
            r = slice(k * ZB, (k + 1) * ZB)
            zsend[it, k, :ZB] = mom[it, 0, r] + ring2[it, 0, r] + ring2[it, 1, r]

        zc = [rdma(zsend.at[it, zo[j]], zrecv.at[it, j], s_z.at[it, j], r_z.at[it, j],
                   at(z_=zo[j])) for j in range(1, NZ)]
        for cpy in zc:
            cpy.start()
        shard = zsend[it, z]
        for j in range(1, NZ):
            zc[j - 1].wait_recv()
            shard += zrecv[it, j]

        xall[it, x] = shard
        xc = [rdma(xall.at[it, x], xall.at[it, x], s_x.at[it, j], r_x.at[it, j], at(x_=xo[j]))
              for j in range(1, NX)]
        for cpy in xc:
            cpy.start()
        for j in range(1, NX):
            xm = (x + NX - j) % NX
            rdma(xall.at[it, xm], xall.at[it, xm], s_x.at[it, j], r_x.at[it, j],
                 at(x_=xo[j])).wait_recv()
        source = xall[it, 0] + xall[it, 1] + xall[it, 2]
        target = xall[it, 3]
        is_target = x == 3
        facing = jnp.where(is_target, source, target)

        zrows = pl.ds(pl.multiple_of(z * ZB, ZB), ZB)
        gath[it, y, zrows] = facing[:ZB]
        gz = [rdma(gath.at[it, y, zrows], gath.at[it, y, zrows], s_gz.at[it, j], r_gz.at[it, j],
                   at(z_=zo[j])) for j in range(1, NZ)]
        for cpy in gz:
            cpy.start()
        source_mass = jnp.sum(source[ZB + 1 : ZB + 2])
        target_mass = jnp.sum(target[ZB + 1 : ZB + 2])
        facing_mass = jnp.where(is_target, source_mass, target_mass)
        marginal = 0.5 * (source[ZB + 1 : ZB + 2] / source_mass
                          + target[ZB + 1 : ZB + 2] / target_mass)
        for j in range(1, NZ):
            zr = pl.ds(pl.multiple_of(((z + NZ - j) % NZ) * ZB, ZB), ZB)
            rdma(gath.at[it, y, zr], gath.at[it, y, zr], s_gz.at[it, j], r_gz.at[it, j],
                 at(z_=zo[j])).wait_recv()
        gu1 = rdma(gath.at[it, y], gath.at[it, y], s_gy.at[it, 0], r_gy.at[it, 0], at(y_=yo[1]))
        gd1 = rdma(gath.at[it, y], gath.at[it, y], s_gy.at[it, 1], r_gy.at[it, 1], at(y_=yo[3]))
        gu1.start()
        gd1.start()
        acc[...] = dot1(pts[y], gath[it, y])

        def got(b, rows, k):
            r = gath.at[it, b, rows]
            rdma(r, r, s_gy.at[it, k], r_gy.at[it, k], at(y_=yo[1])).wait_recv()

        whole, lo, hi = pl.ds(0, YB), pl.ds(0, 128), pl.ds(128, 128)
        got(yo[3], whole, 0)
        gu2 = rdma(gath.at[it, yo[3], lo], gath.at[it, yo[3], lo], s_gy.at[it, 2],
                   r_gy.at[it, 2], at(y_=yo[1]))
        gu2.start()
        got(yo[1], whole, 1)
        gd2 = rdma(gath.at[it, yo[1], hi], gath.at[it, yo[1], hi], s_gy.at[it, 3],
                   r_gy.at[it, 3], at(y_=yo[3]))
        gd2.start()
        acc[...] += dot1(pts[yo[3]], gath[it, yo[3]])
        acc[...] += dot1(pts[yo[1]], gath[it, yo[1]])
        got(yo[2], lo, 2)
        got(yo[2], hi, 3)
        part[it, 0] = acc[oth] + dot1(pts[yo[2], oth], gath[it, yo[2]])
        pc = rdma(part.at[it, 0], part.at[it, 1], s_pt.at[it], r_pt.at[it], at(c_=other))
        pc.start()
        cross = acc[own] + dot1(pts[yo[2], own], gath[it, yo[2]])
        pc.wait_recv()
        cross += part[it, 1]

        facing_columns = facing[ZB + 1 : ZB + 2]
        facing_norms = facing[ZB : ZB + 1]
        squares_own = meta[own, 0:1]
        g = (
            squares_own * (facing_columns / facing_mass)
            - 2.0 * (cross / facing_mass)
            + facing_norms / facing_mass
        ) / marginal
        grad[...] = g
        centred = g - jnp.sum(g, axis=1, keepdims=True) * (1.0 / RANK)
        largest = jnp.max(jnp.abs(centred))

        last = it == ITERS - 1

        @pl.when(last)
        def _():
            @pl.when(swapped)
            def _():
                rdma(lf, fin.at[0], s_fin.at[0], r_fin.at[0], at(c_=vc, x_=xq)).start()
                rdma(grad, fin.at[1], s_fin.at[1], r_fin.at[1], at(c_=vc, x_=xq)).start()

        tile = (8, 128)
        mx[it, 0] = jnp.full(tile, largest)
        mc = [rdma(mx.at[it, 0], mx.at[it, j], s_mc.at[it, j], r_mc.at[it, j],
                   at(c_=cx[j][0], x_=cx[j][1])) for j in range(1, 8)]
        for cpy in mc:
            cpy.start()
        m = mx[it, 0]
        for j in range(1, 8):
            mc[j - 1].wait_recv()
        for j in range(1, 8):
            m = jnp.maximum(m, mx[it, j])
        mx[it, 8] = m
        my = [rdma(mx.at[it, 8], mx.at[it, 8 + j], s_my.at[it, j], r_my.at[it, j], at(y_=yo[j]))
              for j in range(1, NY)]
        for cpy in my:
            cpy.start()
        for cpy in my:
            cpy.wait_recv()
        for j in range(1, NY):
            m = jnp.maximum(m, mx[it, 8 + j])
        mx[it, 12] = m
        mz = [rdma(mx.at[it, 12], mx.at[it, 12 + j], s_mz.at[it, j], r_mz.at[it, j],
                   at(z_=zo[j])) for j in range(1, NZ)]
        for cpy in mz:
            cpy.start()
        for cpy in mz:
            cpy.wait_recv()
        for j in range(1, NZ):
            m = jnp.maximum(m, mx[it, 12 + j])
        rate = STEP_SCALE / (m[0:1, 0:1] + 1e-6)

        @pl.when(jnp.logical_not(last))
        def _():
            lf[...] = lf[...] - rate * grad[...]

        @pl.when(last)
        def _():
            def finish(a, b):
                u = a - rate * b
                ex = jnp.exp(u - jnp.max(u, axis=1, keepdims=True))
                out[...] = RANK * (ex / jnp.sum(ex, axis=1, keepdims=True))

            @pl.when(swapped)
            def _():
                for k, src in ((0, lf), (1, grad)):
                    cpy = rdma(src, fin.at[k], s_fin.at[k], r_fin.at[k], at(c_=vc, x_=xq))
                    cpy.wait_send()
                    cpy.wait_recv()
                finish(fin[0], fin[1])

            @pl.when(jnp.logical_not(swapped))
            def _():
                finish(lf[...], grad[...])

        for cpy in [up1, dn1, up2, dn2, gu1, gd1, gu2, gd2, pc] + st + zc + xc + gz + mc + my + mz:
            cpy.wait_send()
        return 0

    lax.fori_loop(0, ITERS, step, 0)

    for b in order:
        half_out(b).wait_send()
    meta_remote.wait_send()

    @pl.when(swapped)
    def _():
        for b in order:
            half_own(b).wait_send()
        lf_remote.wait_send()
        meta_own.wait_send()


def body(points, log_factor, masses):
    mass = jnp.broadcast_to(masses[:, None], (ROWS, 128))
    f32 = jnp.float32
    vm = lambda *s: pltpu.VMEM(s, f32)
    dma = lambda *s: pltpu.SemaphoreType.DMA(s)
    n = ITERS
    return pl.pallas_call(
        kernel,
        out_shape=jax.ShapeDtypeStruct((ROWS, RANK), f32),
        in_specs=[pl.BlockSpec(memory_space=pltpu.VMEM)] * 3,
        out_specs=pl.BlockSpec(memory_space=pltpu.VMEM),
        scratch_shapes=[
            vm(NY, 2 * ROWS, YB), vm(ROWS, RANK), vm(2 * ROWS, 128), vm(ROWS, 128),
            vm(n, 2 * ROWS, RANK), vm(n, NY, YB, RANK), vm(n, 2, 128, RANK), vm(n, 2, YB, RANK),
            vm(n, NY, 8, RANK), vm(n, NZ, ZS, RANK), vm(n, NZ, ZS, RANK), vm(n, NX, ZS, RANK),
            vm(n, NY, YB, RANK), vm(2 * ROWS, RANK), vm(n, 2, ROWS, RANK),
            vm(n, 20, 8, 128), vm(ROWS, RANK), vm(2, ROWS, RANK),
            dma(2, NY), dma(NY, 2), pltpu.SemaphoreType.DMA, pltpu.SemaphoreType.DMA,
            dma(2), dma(2), dma(n), dma(n), dma(n, 2), dma(n, 2), dma(n, 2), dma(n, 2),
            dma(n, NY), dma(n, NY), dma(n, NZ), dma(n, NZ), dma(n, NX), dma(n, NX),
            dma(n, NZ), dma(n, NZ), dma(n, 4), dma(n, 4), dma(n), dma(n),
            dma(n, 8), dma(n, 8), dma(n, NY), dma(n, NY), dma(n, NZ), dma(n, NZ),
            dma(2), dma(2),
        ],
        compiler_params=pltpu.CompilerParams(
            collective_id=0, has_side_effects=True, vmem_limit_bytes=48 << 20
        ),
        name="steps",
    )(points, log_factor, mass)


def solution(mesh):
    split = Mesh(mesh.devices.reshape(2, 2, 4, 2, 8), AXES)
    rows = ("xl", "c", "y", "xh", "z")
    return jax.shard_map(
        body,
        mesh=split,
        in_specs=(P(rows, None), P(rows, None), P(rows)),
        out_specs=P(rows, None),
        check_vma=False,
    )
```

time: 419 us -> 177 us (0.42); the launches traced: 412 us -> 176 us
  Pallas kernels: 0 us -> 172 us
  waiting for transfers between devices: 164 us -> 0 us
  blocking collectives: 152 us -> 0 us
  starting transfers between devices: 37.9 us -> 0 us
  between operations: 17.5 us -> 0.03 us
  matrix products: 14.3 us -> 0 us
  other arithmetic: 13.1 us -> 0 us
  local copies, waits for them, and re-layouts: 12.7 us -> 4.01 us
    pallas_call x0 -> x1, Pallas kernels: none -> 172 us  [body(): pl.pallas_call(kernel, out_shape=jax.ShapeDtypeStruct((ROWS, RANK), f32),...]
    all_to_all x4 -> x0, waiting for transfers between devices: 100 us -> none  [the longest x2 90 us: summed_on_arrival(): tiles = lax.all_to_all(in_blocks(x, dim, length), axis, 0, 0, tiled=True)]
    all_gather x6 -> x0, blocking collectives: 79.7 us -> none  [the longest x4 52.9 us: all_blocks(): tiles = lax.all_gather(tiles, axes[k])]
    pmax x10 -> x0, blocking collectives: 72.7 us -> none  [by_axis(): return functools.reduce(lax.pmax, axes, x)]
    all_gather x2 -> x0, waiting for transfers between devices: 63.4 us -> none  [all_blocks(): tiles = lax.all_gather(tiles, axes[k])]
    all_to_all x4 -> x0, starting transfers between devices: 37.8 us -> none  [the longest x2 23.6 us: copy_for_each(): return lax.all_to_all(copies, axis, split_axis=0, concat_axis=0, tiled=True)]
    dot_general x6 -> x0, matrix products: 14.3 us -> none  [the longest x2 7.32 us: body(): jnp.dot(points, gather_axes(facing_shard, PTS, (1, 2, 0), 0), precision=h...]
    reduce_sum x13 -> x0, other arithmetic: 7.98 us -> none  [the longest x2 3.46 us: summed_on_arrival(): return jnp.sum(tiles, axis=0)]
  transfers between devices with their start and end apart: 6 -> 0, of which waited for: 6 -> 0; matrix products, arithmetic and copies ran while one was open for 4% -> 0% of each run, Pallas kernels for 0% -> 0%
where the time goes in v1:
time: 177 us; the launch traced here: 176 us
  Pallas kernels  172 us (97%)
  local copies, waits for them, and re-layouts  4.01 us (2%)
    pallas_call x1, Pallas kernels, body(): pl.pallas_call(kernel, out_shape=jax.ShapeDtypeStruct((ROWS, RANK), f32),...  172 us

profile of v1, /device:TPU:1, one launch (start us, length us, event | category | flops | bytes accessed | tf_op | source)
XLA Modules:
  0.0 175.6 jit_solution(16359714462859618926)
XLA Ops:
  0.0 0.8 broadcast_in_dim.2.mass
  0.8 0.0 copy-start
  0.8 1.6 copy-done
  2.4 0.0 copy-start.1
  2.4 0.9 copy-done.1
  3.3 171.6 %steps.1 = f32[256,256]{1,0:T(8,128)S(1)} custom-call(f32[256,2048]{1,0:T(8,128)S(1)} %copy-done, f32[256,256]{1,0:T(8,128)S(1)} %copy-done.1, f32[256,128]{1,0:T(8,128)S(1)} %broadcast_in_dim.2.mass), custom_call_target="tpu_custom_call" | custom-call | tf_op jit(solution)/shard_map/steps/pallas_call | solution.py:370
  174.9 0.7 copy.5
Async XLA Ops:
  0.8 1.6 copy-start
  2.4 0.9 copy-start.1

commit v2 on v1

--- a/solution.py
+++ b/solution.py
@@ -35,10 +35,10 @@
 
 def kernel(
     points, lf_in, mass, out,
-    pts, lf, meta, meta_out, scaled, mom, ring1, ring2, stat, zsend, zrecv, xall, gath, acc, part,
+    pts, pv, relay, lf, meta, meta_out, percol, scaled, mom, ring1, ring2, stat, zsend, zrecv, xall, gath, acc, part,
     mx, grad, fin,
-    s_pts, r_pts, s_lf, r_lf, s_meta, r_meta, s_sc, r_sc, s_r1, r_r1, s_r2, r_r2, s_st, r_st,
-    s_z, r_z, s_x, r_x, s_gz, r_gz, s_gy, r_gy, s_pt, r_pt, s_mc, r_mc, s_my, r_my, s_mz, r_mz,
+    r_pv, s_rel, r_rel, s_fwd, s_pts, r_pts, s_lf, r_lf, s_meta, r_meta, s_sc, r_sc, s_r1, r_r1, s_r2, r_r2, s_st, r_st,
+    s_z, r_z, s_x, r_x, s_gz, r_gz, s_gy, r_gy, s_pt, r_pt, s_mc, r_mc, s_my, r_my,
     s_fin, r_fin,
 ):
     xl, c, y, xh, z = (lax.axis_index(a) for a in AXES)
@@ -64,6 +64,10 @@
     zo = [(z + j) % NZ for j in range(NZ)]
     xo = [(x + j) % NX for j in range(NX)]
     cx = [(c if i == 0 else other, xo[j]) for i in range(2) for j in range(NX)]
+    yz = [(yo[i], zo[j]) for i in range(NY) for j in range(NZ)]
+    own = pl.ds(pl.multiple_of(c * ROWS, ROWS), ROWS)
+    oth = pl.ds(pl.multiple_of(other * ROWS, ROWS), ROWS)
+    relays = x % 2 == 0
 
     def rdma(src, dst, ss, rs, dev):
         return pltpu.make_async_remote_copy(
@@ -71,59 +75,72 @@
             device_id_type=pl.DeviceIdType.MESH,
         )
 
+    load = pltpu.make_async_copy(points, pv, r_pv)
+    load.start()
+    lf_remote = rdma(lf_in, lf, s_lf, r_lf, at(c_=vc, x_=xq))
+    lf_local = pltpu.make_async_copy(lf_in, lf, r_lf)
+    order = [yo[2], yo[1], yo[3], yo[0]]
+
+    def cols(h, b, r, n):
+        return points.at[pl.ds(r, n), pl.ds(pl.multiple_of(h * HALF + b * YB, YB), YB)]
+
+    def half_local(b):
+        return pltpu.make_async_copy(cols(c, b, 0, ROWS), pts.at[b, own], r_pts.at[b, c])
+
+    def half_out(b):
+        return rdma(cols(other, b, 0, ROWS), pts.at[b, own], s_pts.at[0, b], r_pts.at[b, c],
+                    at(c_=other))
+
+    def piece(j, h, r):
+        return rdma(cols(h, order[j], r * 128, 128), relay.at[r, j], s_rel.at[h, r, j],
+                    r_rel.at[r, j], at(c_=h, x_=xo[1] if r == 0 else xo[3]))
+
+    def forward(j, r):
+        to = xo[1] if r == 0 else xo[3]
+        slot = (3 - to) // 2
+        rows = pl.ds(pl.multiple_of(slot * ROWS + r * 128, 128), 128)
+        return rdma(relay.at[r, j], pts.at[order[j], rows], s_fwd.at[r, j],
+                    r_pts.at[order[j], slot], at(x_=to))
+
+    @pl.when(jnp.logical_not(swapped))
+    def _():
+        lf_local.start()
+        for b in order:
+            half_local(b).start()
+
     barrier = pltpu.get_barrier_semaphore()
-    peers = [at(c_=a, x_=b) for a, b in cx[1:]]
-    peers += [at(y_=b) for b in yo[1:]] + [at(z_=b) for b in zo[1:]]
+    peers = [at(c_=a, x_=b) for a, b in cx[1:]] + [at(y_=a, z_=b) for a, b in yz[1:]]
     for p in peers:
         pl.semaphore_signal(barrier, inc=1, device_id=p, device_id_type=pl.DeviceIdType.MESH)
     pl.semaphore_wait(barrier, len(peers))
 
-    def cols(h, b):
-        return points.at[:, pl.ds(pl.multiple_of(h * HALF + b * YB, YB), YB)]
-
-    order = [yo[2], yo[1], yo[3], yo[0]]
-    mine = pl.ds(pl.multiple_of(vc * ROWS, ROWS), ROWS)
-
-    def half_out(b):
-        return rdma(cols(other, b), pts.at[b, mine], s_pts.at[0, b], r_pts.at[b, vc],
-                    at(c_=other, x_=xq))
-
-    def half_own(b):
-        return rdma(cols(c, b), pts.at[b, mine], s_pts.at[1, b], r_pts.at[b, vc],
-                    at(c_=c, x_=xq))
-
-    def half_local(b):
-        return pltpu.make_async_copy(cols(c, b), pts.at[b, mine], r_pts.at[b, vc])
-
-    lf_remote = rdma(lf_in, lf, s_lf, r_lf, at(c_=vc, x_=xq))
-    lf_local = pltpu.make_async_copy(lf_in, lf, r_lf)
-
     @pl.when(swapped)
     def _():
         lf_remote.start()
+        for j in range(NY):
+            for r in range(2):
+                for h in range(2):
+                    piece(j, h, r).start()
+
+    @pl.when(jnp.logical_not(swapped))
+    def _():
         for b in order:
             half_out(b).start()
-            half_own(b).start()
-
-    @pl.when(jnp.logical_not(swapped))
-    def _():
-        lf_local.start()
-        for b in order:
-            half_out(b).start()
-            half_local(b).start()
-
+
+    load.wait()
     squares = jnp.zeros((ROWS, 1), jnp.float32)
     for k in range(8):
-        part_k = points[:, k * 256 : (k + 1) * 256]
+        part_k = pv[:, k * 256 : (k + 1) * 256]
         squares += jnp.sum(part_k * part_k, axis=1, keepdims=True)
-    lane = lax.broadcasted_iota(jnp.int32, (ROWS, 128), 1)
+    squares_row = jnp.transpose(jnp.broadcast_to(squares, (ROWS, 128)))[:8]
+    row = lax.broadcasted_iota(jnp.int32, (8, ROWS), 0)
     meta_out[...] = jnp.where(
-        lane == 0, squares, jnp.where(lane == 1, 1.0, jnp.where(lane == 2, mass[...], 0.0))
+        row == 0, squares_row, jnp.where(row == 1, 1.0, jnp.where(row == 2, mass[...], 0.0))
     )
-    meta_remote = rdma(meta_out, meta.at[mine], s_meta.at[0], r_meta.at[vc],
+    meta_remote = rdma(meta_out, meta.at[vc], s_meta.at[0], r_meta.at[vc],
                        at(c_=other, x_=xq))
-    meta_own = rdma(meta_out, meta.at[mine], s_meta.at[1], r_meta.at[vc], at(c_=c, x_=xq))
-    meta_local = pltpu.make_async_copy(meta_out, meta.at[mine], r_meta.at[vc])
+    meta_own = rdma(meta_out, meta.at[vc], s_meta.at[1], r_meta.at[vc], at(c_=c, x_=xq))
+    meta_local = pltpu.make_async_copy(meta_out, meta.at[vc], r_meta.at[vc])
     meta_remote.start()
 
     @pl.when(swapped)
@@ -134,22 +151,20 @@
     def _():
         meta_local.start()
 
-    own = pl.ds(pl.multiple_of(c * ROWS, ROWS), ROWS)
-    oth = pl.ds(pl.multiple_of(other * ROWS, ROWS), ROWS)
     lf_remote.wait_recv()
     for v in range(2):
-        rdma(meta_out, meta.at[pl.ds(v * ROWS, ROWS)], s_meta.at[0], r_meta.at[v],
-             at(c_=other)).wait_recv()
+        rdma(meta_out, meta.at[v], s_meta.at[0], r_meta.at[v], at(c_=other)).wait_recv()
+    percol[...] = jnp.transpose(meta[c])
 
     def wait_points(b):
         for v in range(2):
-            rdma(cols(c, b), pts.at[b, pl.ds(v * ROWS, ROWS)], s_pts.at[0, b], r_pts.at[b, v],
-                 at(c_=other)).wait_recv()
+            dst = pts.at[b, pl.ds(v * ROWS, ROWS)]
+            rdma(dst, dst, s_pts.at[0, b], r_pts.at[b, v], at(c_=other)).wait_recv()
 
     def step(it, _):
         v = lf[...]
         e = jnp.exp(v - jnp.max(v, axis=1, keepdims=True))
-        mass_own = meta[own, 2:3]
+        mass_own = percol[:, 2:3]
         scaled[it, own] = e / jnp.sum(e, axis=1, keepdims=True) * mass_own
         cp = rdma(scaled.at[it, own], scaled.at[it, own], s_sc.at[it], r_sc.at[it], at(c_=other))
         cp.start()
@@ -157,38 +172,43 @@
         rdma(scaled.at[it, oth], scaled.at[it, oth], s_sc.at[it], r_sc.at[it],
              at(c_=other)).wait_recv()
 
-        stat[it, 0] = dot0(meta[...], scaled[it])[:8]
+        stat[it, 0] = dot1(meta[0], scaled[it, :ROWS]) + dot1(meta[1], scaled[it, ROWS:])
         st = [rdma(stat.at[it, 0], stat.at[it, j], s_st.at[it, j], r_st.at[it, j], at(y_=yo[j]))
               for j in range(1, NY)]
         for cpy in st:
             cpy.start()
 
-        def moment(b):
+        def moment(j):
             @pl.when(it == 0)
             def _():
-                wait_points(b)
-            return dot0(pts[b], scaled[it])
-
-        mom[it, 2] = moment(yo[2])
+                @pl.when(relays)
+                def _():
+                    for r in range(2):
+                        piece(j, c, r).wait_recv()
+                        forward(j, r).start()
+                wait_points(order[j])
+            return dot0(pts[order[j]], scaled[it])
+
+        mom[it, 2] = moment(0)
         up1 = rdma(mom.at[it, 2, pl.ds(0, 128)], ring1.at[it, 0], s_r1.at[it, 0],
                    r_r1.at[it, 0], at(y_=yo[1]))
         dn1 = rdma(mom.at[it, 2, pl.ds(128, 128)], ring1.at[it, 1], s_r1.at[it, 1],
                    r_r1.at[it, 1], at(y_=yo[3]))
         up1.start()
         dn1.start()
-        m1 = moment(yo[1])
+        m1 = moment(1)
         up1.wait_recv()
         mom[it, 1, :128] = m1[:128] + ring1[it, 0]
         mom[it, 1, 128:] = m1[128:]
         up2 = rdma(mom.at[it, 1], ring2.at[it, 0], s_r2.at[it, 0], r_r2.at[it, 0], at(y_=yo[1]))
         up2.start()
-        m3 = moment(yo[3])
+        m3 = moment(2)
         dn1.wait_recv()
         mom[it, 3, :128] = m3[:128]
         mom[it, 3, 128:] = m3[128:] + ring1[it, 1]
         dn2 = rdma(mom.at[it, 3], ring2.at[it, 1], s_r2.at[it, 1], r_r2.at[it, 1], at(y_=yo[3]))
         dn2.start()
-        mom[it, 0] = moment(yo[0])
+        mom[it, 0] = moment(3)
         for cpy in st:
             cpy.wait_recv()
         stats_y = stat[it, 0] + stat[it, 1] + stat[it, 2] + stat[it, 3]
@@ -270,7 +290,7 @@
 
         facing_columns = facing[ZB + 1 : ZB + 2]
         facing_norms = facing[ZB : ZB + 1]
-        squares_own = meta[own, 0:1]
+        squares_own = percol[:, 0:1]
         g = (
             squares_own * (facing_columns / facing_mass)
             - 2.0 * (cross / facing_mass)
@@ -301,23 +321,14 @@
         for j in range(1, 8):
             m = jnp.maximum(m, mx[it, j])
         mx[it, 8] = m
-        my = [rdma(mx.at[it, 8], mx.at[it, 8 + j], s_my.at[it, j], r_my.at[it, j], at(y_=yo[j]))
-              for j in range(1, NY)]
+        my = [rdma(mx.at[it, 8], mx.at[it, 8 + j], s_my.at[it, j], r_my.at[it, j],
+                   at(y_=yz[j][0], z_=yz[j][1])) for j in range(1, NY * NZ)]
         for cpy in my:
             cpy.start()
         for cpy in my:
             cpy.wait_recv()
-        for j in range(1, NY):
+        for j in range(1, NY * NZ):
             m = jnp.maximum(m, mx[it, 8 + j])
-        mx[it, 12] = m
-        mz = [rdma(mx.at[it, 12], mx.at[it, 12 + j], s_mz.at[it, j], r_mz.at[it, j],
-                   at(z_=zo[j])) for j in range(1, NZ)]
-        for cpy in mz:
-            cpy.start()
-        for cpy in mz:
-            cpy.wait_recv()
-        for j in range(1, NZ):
-            m = jnp.maximum(m, mx[it, 12 + j])
         rate = STEP_SCALE / (m[0:1, 0:1] + 1e-6)
 
         @pl.when(jnp.logical_not(last))
@@ -329,7 +340,7 @@
             def finish(a, b):
                 u = a - rate * b
                 ex = jnp.exp(u - jnp.max(u, axis=1, keepdims=True))
-                out[...] = RANK * (ex / jnp.sum(ex, axis=1, keepdims=True))
+                out[...] = ex / jnp.sum(ex, axis=1, keepdims=True)
 
             @pl.when(swapped)
             def _():
@@ -343,53 +354,68 @@
             def _():
                 finish(lf[...], grad[...])
 
-        for cpy in [up1, dn1, up2, dn2, gu1, gd1, gu2, gd2, pc] + st + zc + xc + gz + mc + my + mz:
+        for cpy in [up1, dn1, up2, dn2, gu1, gd1, gu2, gd2, pc] + st + zc + xc + gz + mc + my:
             cpy.wait_send()
         return 0
 
     lax.fori_loop(0, ITERS, step, 0)
 
-    for b in order:
-        half_out(b).wait_send()
     meta_remote.wait_send()
 
     @pl.when(swapped)
     def _():
-        for b in order:
-            half_own(b).wait_send()
         lf_remote.wait_send()
         meta_own.wait_send()
+        for j in range(NY):
+            for r in range(2):
+                for h in range(2):
+                    piece(j, h, r).wait_send()
+
+    @pl.when(jnp.logical_not(swapped))
+    def _():
+        for b in order:
+            half_out(b).wait_send()
+
+    @pl.when(relays)
+    def _():
+        for j in range(NY):
+            for r in range(2):
+                forward(j, r).wait_send()
 
 
 def body(points, log_factor, masses):
-    mass = jnp.broadcast_to(masses[:, None], (ROWS, 128))
+    mass = masses.reshape(1, ROWS)
     f32 = jnp.float32
     vm = lambda *s: pltpu.VMEM(s, f32)
     dma = lambda *s: pltpu.SemaphoreType.DMA(s)
     n = ITERS
-    return pl.pallas_call(
+    share = pl.pallas_call(
         kernel,
         out_shape=jax.ShapeDtypeStruct((ROWS, RANK), f32),
-        in_specs=[pl.BlockSpec(memory_space=pltpu.VMEM)] * 3,
+        in_specs=[pl.BlockSpec(memory_space=pltpu.HBM)] * 2
+        + [pl.BlockSpec(memory_space=pltpu.VMEM)],
         out_specs=pl.BlockSpec(memory_space=pltpu.VMEM),
         scratch_shapes=[
-            vm(NY, 2 * ROWS, YB), vm(ROWS, RANK), vm(2 * ROWS, 128), vm(ROWS, 128),
+            vm(NY, 2 * ROWS, YB), vm(ROWS, 2 * HALF), vm(2, NY, 128, YB), vm(ROWS, RANK),
+            vm(2, 8, ROWS), vm(8, ROWS), vm(ROWS, 8),
             vm(n, 2 * ROWS, RANK), vm(n, NY, YB, RANK), vm(n, 2, 128, RANK), vm(n, 2, YB, RANK),
             vm(n, NY, 8, RANK), vm(n, NZ, ZS, RANK), vm(n, NZ, ZS, RANK), vm(n, NX, ZS, RANK),
             vm(n, NY, YB, RANK), vm(2 * ROWS, RANK), vm(n, 2, ROWS, RANK),
-            vm(n, 20, 8, 128), vm(ROWS, RANK), vm(2, ROWS, RANK),
+            vm(n, 40, 8, 128), vm(ROWS, RANK), vm(2, ROWS, RANK),
+            pltpu.SemaphoreType.DMA, dma(2, 2, NY), dma(2, NY), dma(2, NY),
             dma(2, NY), dma(NY, 2), pltpu.SemaphoreType.DMA, pltpu.SemaphoreType.DMA,
             dma(2), dma(2), dma(n), dma(n), dma(n, 2), dma(n, 2), dma(n, 2), dma(n, 2),
             dma(n, NY), dma(n, NY), dma(n, NZ), dma(n, NZ), dma(n, NX), dma(n, NX),
             dma(n, NZ), dma(n, NZ), dma(n, 4), dma(n, 4), dma(n), dma(n),
-            dma(n, 8), dma(n, 8), dma(n, NY), dma(n, NY), dma(n, NZ), dma(n, NZ),
+            dma(n, 8), dma(n, 8), dma(n, NY * NZ), dma(n, NY * NZ),
             dma(2), dma(2),
         ],
         compiler_params=pltpu.CompilerParams(
-            collective_id=0, has_side_effects=True, vmem_limit_bytes=48 << 20
+            collective_id=0, has_side_effects=True, vmem_limit_bytes=62 << 20
         ),
         name="steps",
     )(points, log_factor, mass)
+    return RANK * share
 
 
 def solution(mesh):

time: 177 us -> 162 us (0.915)
  Pallas kernels: 172 us -> 159 us
  local copies, waits for them, and re-layouts: 4.01 us -> 0 us
    pallas_call x1, Pallas kernels: 172 us -> 159 us  [body(): pl.pallas_call(kernel, out_shape=jax.ShapeDtypeStruct((ROWS, RANK), f32),...]
    unnamed x5 -> x0, local copies, waits for them, and re-layouts: 3.24 us -> none
where the time goes in v2:
time: 162 us; the launch traced here: 160 us
  Pallas kernels  159 us (98%)
  other arithmetic  1.67 us (1%)
    pallas_call x1, Pallas kernels, body(): pl.pallas_call(kernel, out_shape=jax.ShapeDtypeStruct((ROWS, RANK), f32),...  159 us

profile of v2, /device:TPU:1, one launch (start us, length us, event | category | flops | bytes accessed | tf_op | source)
XLA Modules:
  0.0 160.5 jit_solution(9705880826834585105)
XLA Ops:
  0.0 158.8 %steps.1 = f32[256,256]{1,0:T(8,128)} custom-call(f32[256,2048]{1,0:T(8,128)} %points.1, f32[256,256]{1,0:T(8,128)} %lf_in.1, f32[1,256]{1,0:T(1,128)} %bitcast.1), custom_call_target="tpu_custom_call" | custom-call | tf_op jit(solution)/shard_map/steps/pallas_call | solution.py:392
  158.8 1.7 %broadcast_multiply_fusion = f32[256,256]{1,0:T(8,128)} fusion(f32[256,256]{1,0:T(8,128)} %steps.1), kind=kLoop, calls=%fused_computation | loop fusion | flops 65536 | bytes 524288 | tf_op jit(solution)/shard_map/mul | solution.py:418

commit v3 on v2

--- a/solution.py
+++ b/solution.py
@@ -37,7 +37,7 @@
     points, lf_in, mass, out,
     pts, pv, relay, lf, meta, meta_out, percol, scaled, mom, ring1, ring2, stat, zsend, zrecv, xall, gath, acc, part,
     mx, grad, fin,
-    r_pv, s_rel, r_rel, s_fwd, s_pts, r_pts, s_lf, r_lf, s_meta, r_meta, s_sc, r_sc, s_r1, r_r1, s_r2, r_r2, s_st, r_st,
+    r_pv, s_rel, r_rel, s_fwd, s_pts, r_pts, s_lf, r_lf, s_meta, r_meta, s_sc, r_sc, s_r, r_r, s_st, r_st,
     s_z, r_z, s_x, r_x, s_gz, r_gz, s_gy, r_gy, s_pt, r_pt, s_mc, r_mc, s_my, r_my,
     s_fin, r_fin,
 ):
@@ -75,6 +75,12 @@
             device_id_type=pl.DeviceIdType.MESH,
         )
 
+    def sent(ref, sem):
+        rdma(ref, ref, sem, sem, at(c_=other)).wait_send()
+
+    def arrived(ref, sem):
+        rdma(ref, ref, sem, sem, at(c_=other)).wait_recv()
+
     load = pltpu.make_async_copy(points, pv, r_pv)
     load.start()
     lf_remote = rdma(lf_in, lf, s_lf, r_lf, at(c_=vc, x_=xq))
@@ -112,20 +118,6 @@
     peers = [at(c_=a, x_=b) for a, b in cx[1:]] + [at(y_=a, z_=b) for a, b in yz[1:]]
     for p in peers:
         pl.semaphore_signal(barrier, inc=1, device_id=p, device_id_type=pl.DeviceIdType.MESH)
-    pl.semaphore_wait(barrier, len(peers))
-
-    @pl.when(swapped)
-    def _():
-        lf_remote.start()
-        for j in range(NY):
-            for r in range(2):
-                for h in range(2):
-                    piece(j, h, r).start()
-
-    @pl.when(jnp.logical_not(swapped))
-    def _():
-        for b in order:
-            half_out(b).start()
 
     load.wait()
     squares = jnp.zeros((ROWS, 1), jnp.float32)
@@ -137,6 +129,8 @@
     meta_out[...] = jnp.where(
         row == 0, squares_row, jnp.where(row == 1, 1.0, jnp.where(row == 2, mass[...], 0.0))
     )
+    pl.semaphore_wait(barrier, len(peers))
+
     meta_remote = rdma(meta_out, meta.at[vc], s_meta.at[0], r_meta.at[vc],
                        at(c_=other, x_=xq))
     meta_own = rdma(meta_out, meta.at[vc], s_meta.at[1], r_meta.at[vc], at(c_=c, x_=xq))
@@ -150,6 +144,19 @@
     @pl.when(jnp.logical_not(swapped))
     def _():
         meta_local.start()
+
+    @pl.when(swapped)
+    def _():
+        lf_remote.start()
+        for j in range(NY):
+            for r in range(2):
+                for h in range(2):
+                    piece(j, h, r).start()
+
+    @pl.when(jnp.logical_not(swapped))
+    def _():
+        for b in order:
+            half_out(b).start()
 
     lf_remote.wait_recv()
     for v in range(2):
@@ -168,17 +175,8 @@
         scaled[it, own] = e / jnp.sum(e, axis=1, keepdims=True) * mass_own
         cp = rdma(scaled.at[it, own], scaled.at[it, own], s_sc.at[it], r_sc.at[it], at(c_=other))
         cp.start()
-        cp.wait_send()
-        rdma(scaled.at[it, oth], scaled.at[it, oth], s_sc.at[it], r_sc.at[it],
-             at(c_=other)).wait_recv()
-
-        stat[it, 0] = dot1(meta[0], scaled[it, :ROWS]) + dot1(meta[1], scaled[it, ROWS:])
-        st = [rdma(stat.at[it, 0], stat.at[it, j], s_st.at[it, j], r_st.at[it, j], at(y_=yo[j]))
-              for j in range(1, NY)]
-        for cpy in st:
-            cpy.start()
-
-        def moment(j):
+
+        def ready(j):
             @pl.when(it == 0)
             def _():
                 @pl.when(relays)
@@ -187,57 +185,62 @@
                         piece(j, c, r).wait_recv()
                         forward(j, r).start()
                 wait_points(order[j])
+
+        def moment(j):
+            ready(j)
             return dot0(pts[order[j]], scaled[it])
 
-        mom[it, 2] = moment(0)
-        up1 = rdma(mom.at[it, 2, pl.ds(0, 128)], ring1.at[it, 0], s_r1.at[it, 0],
-                   r_r1.at[it, 0], at(y_=yo[1]))
-        dn1 = rdma(mom.at[it, 2, pl.ds(128, 128)], ring1.at[it, 1], s_r1.at[it, 1],
-                   r_r1.at[it, 1], at(y_=yo[3]))
-        up1.start()
-        dn1.start()
-        m1 = moment(1)
+        lo, hi = pl.ds(0, 128), pl.ds(128, 128)
+        up, dn = at(y_=yo[1]), at(y_=yo[3])
+        ready(0)
+        mom[it, 2] = dot0(pts[order[0], own], scaled[it, own])
+        arrived(scaled.at[it, oth], r_sc.at[it])
+        mom[it, 2] += dot0(pts[order[0], oth], scaled[it, oth])
+
+        def ring(k, rows, dst, n, dev):
+            cpy = rdma(mom.at[it, k, rows], dst, s_r.at[it, n], r_r.at[it, n], dev)
+            cpy.start()
+            return cpy
+
+        up1 = ring(2, lo, ring1.at[it, 0], 0, up)
+        dn1 = ring(2, hi, ring1.at[it, 1], 1, dn)
+        mom[it, 1] = moment(1)
+        up2 = ring(1, hi, ring2.at[it, 0, hi], 2, up)
+        mom[it, 3] = moment(2)
+        dn2 = ring(3, lo, ring2.at[it, 1, lo], 3, dn)
         up1.wait_recv()
-        mom[it, 1, :128] = m1[:128] + ring1[it, 0]
-        mom[it, 1, 128:] = m1[128:]
-        up2 = rdma(mom.at[it, 1], ring2.at[it, 0], s_r2.at[it, 0], r_r2.at[it, 0], at(y_=yo[1]))
-        up2.start()
-        m3 = moment(2)
+        mom[it, 1, lo] += ring1[it, 0]
+        up3 = ring(1, lo, ring2.at[it, 0, lo], 4, up)
         dn1.wait_recv()
-        mom[it, 3, :128] = m3[:128]
-        mom[it, 3, 128:] = m3[128:] + ring1[it, 1]
-        dn2 = rdma(mom.at[it, 3], ring2.at[it, 1], s_r2.at[it, 1], r_r2.at[it, 1], at(y_=yo[3]))
-        dn2.start()
+        mom[it, 3, hi] += ring1[it, 1]
+        dn3 = ring(3, hi, ring2.at[it, 1, hi], 5, dn)
+
+        stat[it, 0] = dot1(meta[0], scaled[it, :ROWS]) + dot1(meta[1], scaled[it, ROWS:])
+        for j in range(1, NY):
+            rdma(stat.at[it, 0], stat.at[it, j], s_st.at[it], r_st.at[it], at(y_=yo[j])).start()
         mom[it, 0] = moment(3)
-        for cpy in st:
-            cpy.wait_recv()
+        arrived(stat.at[it, pl.ds(1, NY - 1)], r_st.at[it])
         stats_y = stat[it, 0] + stat[it, 1] + stat[it, 2] + stat[it, 3]
         for k in range(NZ):
             zsend[it, k, ZB:] = stats_y
-        up2.wait_recv()
-        dn2.wait_recv()
+        for cpy in (up2, dn2, up3, dn3):
+            cpy.wait_recv()
         for k in range(NZ):
             r = slice(k * ZB, (k + 1) * ZB)
             zsend[it, k, :ZB] = mom[it, 0, r] + ring2[it, 0, r] + ring2[it, 1, r]
 
-        zc = [rdma(zsend.at[it, zo[j]], zrecv.at[it, j], s_z.at[it, j], r_z.at[it, j],
-                   at(z_=zo[j])) for j in range(1, NZ)]
-        for cpy in zc:
-            cpy.start()
+        for j in range(1, NZ):
+            rdma(zsend.at[it, zo[j]], zrecv.at[it, j], s_z.at[it], r_z.at[it],
+                 at(z_=zo[j])).start()
+        arrived(zrecv.at[it, pl.ds(1, NZ - 1)], r_z.at[it])
         shard = zsend[it, z]
         for j in range(1, NZ):
-            zc[j - 1].wait_recv()
             shard += zrecv[it, j]
 
         xall[it, x] = shard
-        xc = [rdma(xall.at[it, x], xall.at[it, x], s_x.at[it, j], r_x.at[it, j], at(x_=xo[j]))
-              for j in range(1, NX)]
-        for cpy in xc:
-            cpy.start()
         for j in range(1, NX):
-            xm = (x + NX - j) % NX
-            rdma(xall.at[it, xm], xall.at[it, xm], s_x.at[it, j], r_x.at[it, j],
-                 at(x_=xo[j])).wait_recv()
+            rdma(xall.at[it, x], xall.at[it, x], s_x.at[it], r_x.at[it], at(x_=xo[j])).start()
+        arrived(xall.at[it, pl.ds(0, NX - 1)], r_x.at[it])
         source = xall[it, 0] + xall[it, 1] + xall[it, 2]
         target = xall[it, 3]
         is_target = x == 3
@@ -245,42 +248,37 @@
 
         zrows = pl.ds(pl.multiple_of(z * ZB, ZB), ZB)
         gath[it, y, zrows] = facing[:ZB]
-        gz = [rdma(gath.at[it, y, zrows], gath.at[it, y, zrows], s_gz.at[it, j], r_gz.at[it, j],
-                   at(z_=zo[j])) for j in range(1, NZ)]
-        for cpy in gz:
-            cpy.start()
+        for j in range(1, NZ):
+            rdma(gath.at[it, y, zrows], gath.at[it, y, zrows], s_gz.at[it], r_gz.at[it],
+                 at(z_=zo[j])).start()
         source_mass = jnp.sum(source[ZB + 1 : ZB + 2])
         target_mass = jnp.sum(target[ZB + 1 : ZB + 2])
         facing_mass = jnp.where(is_target, source_mass, target_mass)
         marginal = 0.5 * (source[ZB + 1 : ZB + 2] / source_mass
                           + target[ZB + 1 : ZB + 2] / target_mass)
-        for j in range(1, NZ):
-            zr = pl.ds(pl.multiple_of(((z + NZ - j) % NZ) * ZB, ZB), ZB)
-            rdma(gath.at[it, y, zr], gath.at[it, y, zr], s_gz.at[it, j], r_gz.at[it, j],
-                 at(z_=zo[j])).wait_recv()
-        gu1 = rdma(gath.at[it, y], gath.at[it, y], s_gy.at[it, 0], r_gy.at[it, 0], at(y_=yo[1]))
-        gd1 = rdma(gath.at[it, y], gath.at[it, y], s_gy.at[it, 1], r_gy.at[it, 1], at(y_=yo[3]))
-        gu1.start()
-        gd1.start()
+        arrived(gath.at[it, y, pl.ds(0, (NZ - 1) * ZB)], r_gz.at[it])
+
+        def block(b, rows, n, dev):
+            ref = gath.at[it, b, rows]
+            return rdma(ref, ref, s_gy.at[it, n], r_gy.at[it, n], dev)
+
+        gout = [block(y, lo, 0, up), block(y, hi, 1, dn), block(y, hi, 2, up),
+                block(y, lo, 3, dn)]
+        for cpy in gout:
+            cpy.start()
         acc[...] = dot1(pts[y], gath[it, y])
-
-        def got(b, rows, k):
-            r = gath.at[it, b, rows]
-            rdma(r, r, s_gy.at[it, k], r_gy.at[it, k], at(y_=yo[1])).wait_recv()
-
-        whole, lo, hi = pl.ds(0, YB), pl.ds(0, 128), pl.ds(128, 128)
-        got(yo[3], whole, 0)
-        gu2 = rdma(gath.at[it, yo[3], lo], gath.at[it, yo[3], lo], s_gy.at[it, 2],
-                   r_gy.at[it, 2], at(y_=yo[1]))
-        gu2.start()
-        got(yo[1], whole, 1)
-        gd2 = rdma(gath.at[it, yo[1], hi], gath.at[it, yo[1], hi], s_gy.at[it, 3],
-                   r_gy.at[it, 3], at(y_=yo[3]))
-        gd2.start()
+        block(yo[3], lo, 0, up).wait_recv()
+        gout += [block(yo[3], lo, 4, up)]
+        gout[4].start()
+        block(yo[1], hi, 1, dn).wait_recv()
+        gout += [block(yo[1], hi, 5, dn)]
+        gout[5].start()
+        block(yo[3], hi, 2, up).wait_recv()
         acc[...] += dot1(pts[yo[3]], gath[it, yo[3]])
+        block(yo[1], lo, 3, dn).wait_recv()
         acc[...] += dot1(pts[yo[1]], gath[it, yo[1]])
-        got(yo[2], lo, 2)
-        got(yo[2], hi, 3)
+        block(yo[2], lo, 4, up).wait_recv()
+        block(yo[2], hi, 5, dn).wait_recv()
         part[it, 0] = acc[oth] + dot1(pts[yo[2], oth], gath[it, yo[2]])
         pc = rdma(part.at[it, 0], part.at[it, 1], s_pt.at[it], r_pt.at[it], at(c_=other))
         pc.start()
@@ -311,24 +309,25 @@
 
         tile = (8, 128)
         mx[it, 0] = jnp.full(tile, largest)
-        mc = [rdma(mx.at[it, 0], mx.at[it, j], s_mc.at[it, j], r_mc.at[it, j],
-                   at(c_=cx[j][0], x_=cx[j][1])) for j in range(1, 8)]
-        for cpy in mc:
-            cpy.start()
-        m = mx[it, 0]
         for j in range(1, 8):
-            mc[j - 1].wait_recv()
-        for j in range(1, 8):
-            m = jnp.maximum(m, mx[it, j])
-        mx[it, 8] = m
-        my = [rdma(mx.at[it, 8], mx.at[it, 8 + j], s_my.at[it, j], r_my.at[it, j],
-                   at(y_=yz[j][0], z_=yz[j][1])) for j in range(1, NY * NZ)]
-        for cpy in my:
-            cpy.start()
-        for cpy in my:
-            cpy.wait_recv()
+            rdma(mx.at[it, 0], mx.at[it, j], s_mc.at[it], r_mc.at[it],
+                 at(c_=cx[j][0], x_=cx[j][1])).start()
+        for cpy in [cp, up1, dn1, up2, dn2, up3, dn3]:
+            cpy.wait_send()
+        sent(stat.at[it, pl.ds(1, NY - 1)], s_st.at[it])
+        sent(zrecv.at[it, pl.ds(1, NZ - 1)], s_z.at[it])
+        arrived(mx.at[it, pl.ds(1, 7)], r_mc.at[it])
+        mx[it, 8] = jnp.max(mx[it, :8], axis=0)
         for j in range(1, NY * NZ):
-            m = jnp.maximum(m, mx[it, 8 + j])
+            rdma(mx.at[it, 8], mx.at[it, 8 + j], s_my.at[it], r_my.at[it],
+                 at(y_=yz[j][0], z_=yz[j][1])).start()
+        sent(xall.at[it, pl.ds(0, NX - 1)], s_x.at[it])
+        sent(gath.at[it, y, pl.ds(0, (NZ - 1) * ZB)], s_gz.at[it])
+        for cpy in gout + [pc]:
+            cpy.wait_send()
+        sent(mx.at[it, pl.ds(1, 7)], s_mc.at[it])
+        arrived(mx.at[it, pl.ds(9, NY * NZ - 1)], r_my.at[it])
+        m = jnp.max(mx[it, 8:40], axis=0)
         rate = STEP_SCALE / (m[0:1, 0:1] + 1e-6)
 
         @pl.when(jnp.logical_not(last))
@@ -354,8 +353,7 @@
             def _():
                 finish(lf[...], grad[...])
 
-        for cpy in [up1, dn1, up2, dn2, gu1, gd1, gu2, gd2, pc] + st + zc + xc + gz + mc + my:
-            cpy.wait_send()
+        sent(mx.at[it, pl.ds(9, NY * NZ - 1)], s_my.at[it])
         return 0
 
     lax.fori_loop(0, ITERS, step, 0)
@@ -404,11 +402,9 @@
             vm(n, 40, 8, 128), vm(ROWS, RANK), vm(2, ROWS, RANK),
             pltpu.SemaphoreType.DMA, dma(2, 2, NY), dma(2, NY), dma(2, NY),
             dma(2, NY), dma(NY, 2), pltpu.SemaphoreType.DMA, pltpu.SemaphoreType.DMA,
-            dma(2), dma(2), dma(n), dma(n), dma(n, 2), dma(n, 2), dma(n, 2), dma(n, 2),
-            dma(n, NY), dma(n, NY), dma(n, NZ), dma(n, NZ), dma(n, NX), dma(n, NX),
-            dma(n, NZ), dma(n, NZ), dma(n, 4), dma(n, 4), dma(n), dma(n),
-            dma(n, 8), dma(n, 8), dma(n, NY * NZ), dma(n, NY * NZ),
-            dma(2), dma(2),
+            dma(2), dma(2), dma(n), dma(n), dma(n, 6), dma(n, 6), dma(n), dma(n),
+            dma(n), dma(n), dma(n), dma(n), dma(n), dma(n), dma(n, 6), dma(n, 6),
+            dma(n), dma(n), dma(n), dma(n), dma(n), dma(n), dma(2), dma(2),
         ],
         compiler_params=pltpu.CompilerParams(
             collective_id=0, has_side_effects=True, vmem_limit_bytes=62 << 20

time: 162 us -> 148 us (0.914)
  Pallas kernels: 159 us -> 146 us
    pallas_call x1, Pallas kernels: 159 us -> 146 us  [body(): pl.pallas_call(kernel, out_shape=jax.ShapeDtypeStruct((ROWS, RANK), f32),...]
where the time goes in v3:
time: 148 us
  Pallas kernels  146 us (99%)
  other arithmetic  1.67 us (1%)
    pallas_call x1, Pallas kernels, body(): pl.pallas_call(kernel, out_shape=jax.ShapeDtypeStruct((ROWS, RANK), f32),...  146 us

profile of v3, /device:TPU:1, one launch (start us, length us, event | category | flops | bytes accessed | tf_op | source)
XLA Modules:
  0.0 147.9 jit_solution(6388607385760762849)
XLA Ops:
  0.0 146.2 %steps.1 = f32[256,256]{1,0:T(8,128)} custom-call(f32[256,2048]{1,0:T(8,128)} %points.1, f32[256,256]{1,0:T(8,128)} %lf_in.1, f32[1,256]{1,0:T(1,128)} %bitcast.1), custom_call_target="tpu_custom_call" | custom-call | tf_op jit(solution)/shard_map/steps/pallas_call | solution.py:390
  146.2 1.7 %broadcast_multiply_fusion = f32[256,256]{1,0:T(8,128)} fusion(f32[256,256]{1,0:T(8,128)} %steps.1), kind=kLoop, calls=%fused_computation | loop fusion | flops 65536 | bytes 524288 | tf_op jit(solution)/shard_map/mul | solution.py:414

commit v4 on v3

--- a/solution.py
+++ b/solution.py
@@ -35,7 +35,7 @@
 
 def kernel(
     points, lf_in, mass, out,
-    pts, pv, relay, lf, meta, meta_out, percol, scaled, mom, ring1, ring2, stat, zsend, zrecv, xall, gath, acc, part,
+    pts, pv, relay, lf, meta, meta_out, percol, scaled, mom, ring1, ring2, stat, statz, zsend, zrecv, xall, gath, acc, part,
     mx, grad, fin,
     r_pv, s_rel, r_rel, s_fwd, s_pts, r_pts, s_lf, r_lf, s_meta, r_meta, s_sc, r_sc, s_r, r_r, s_st, r_st,
     s_z, r_z, s_x, r_x, s_gz, r_gz, s_gy, r_gy, s_pt, r_pt, s_mc, r_mc, s_my, r_my,
@@ -145,13 +145,23 @@
     def _():
         meta_local.start()
 
+    def each_piece(j, act):
+        for r in range(2):
+            for h in range(2):
+                act(piece(j, h, r))
+
+    def start(cpy):
+        cpy.start()
+
+    def wait_send(cpy):
+        cpy.wait_send()
+
     @pl.when(swapped)
     def _():
         lf_remote.start()
-        for j in range(NY):
-            for r in range(2):
-                for h in range(2):
-                    piece(j, h, r).start()
+        each_piece(0, start)
+        lf_remote.wait_send()
+        each_piece(1, start)
 
     @pl.when(jnp.logical_not(swapped))
     def _():
@@ -175,6 +185,13 @@
         scaled[it, own] = e / jnp.sum(e, axis=1, keepdims=True) * mass_own
         cp = rdma(scaled.at[it, own], scaled.at[it, own], s_sc.at[it], r_sc.at[it], at(c_=other))
         cp.start()
+        last = it == ITERS - 1
+
+        @pl.when(last)
+        def _():
+            @pl.when(swapped)
+            def _():
+                rdma(lf, fin.at[0], s_fin.at[0], r_fin.at[0], at(c_=vc, x_=xq)).start()
 
         def ready(j):
             @pl.when(it == 0)
@@ -184,6 +201,13 @@
                     for r in range(2):
                         piece(j, c, r).wait_recv()
                         forward(j, r).start()
+
+                if j < 2:
+                    @pl.when(swapped)
+                    def _():
+                        each_piece(j, wait_send)
+                        each_piece(j + 2, start)
+
                 wait_points(order[j])
 
         def moment(j):
@@ -208,6 +232,10 @@
         up2 = ring(1, hi, ring2.at[it, 0, hi], 2, up)
         mom[it, 3] = moment(2)
         dn2 = ring(3, lo, ring2.at[it, 1, lo], 3, dn)
+        stat[it, 0] = dot1(meta[0], scaled[it, :ROWS]) + dot1(meta[1], scaled[it, ROWS:])
+        for j in range(1, NY):
+            rdma(stat.at[it, 0], stat.at[it, j], s_st.at[it, 0], r_st.at[it, 0],
+                 at(y_=yo[j])).start()
         up1.wait_recv()
         mom[it, 1, lo] += ring1[it, 0]
         up3 = ring(1, lo, ring2.at[it, 0, lo], 4, up)
@@ -215,19 +243,18 @@
         mom[it, 3, hi] += ring1[it, 1]
         dn3 = ring(3, hi, ring2.at[it, 1, hi], 5, dn)
 
-        stat[it, 0] = dot1(meta[0], scaled[it, :ROWS]) + dot1(meta[1], scaled[it, ROWS:])
-        for j in range(1, NY):
-            rdma(stat.at[it, 0], stat.at[it, j], s_st.at[it], r_st.at[it], at(y_=yo[j])).start()
         mom[it, 0] = moment(3)
-        arrived(stat.at[it, pl.ds(1, NY - 1)], r_st.at[it])
-        stats_y = stat[it, 0] + stat[it, 1] + stat[it, 2] + stat[it, 3]
-        for k in range(NZ):
-            zsend[it, k, ZB:] = stats_y
+
+        arrived(stat.at[it, pl.ds(1, NY - 1)], r_st.at[it, 0])
+        statz[it, 0] = stat[it, 0] + stat[it, 1] + stat[it, 2] + stat[it, 3]
+        for j in range(1, NZ):
+            rdma(statz.at[it, 0], statz.at[it, j], s_st.at[it, 1], r_st.at[it, 1],
+                 at(z_=zo[j])).start()
         for cpy in (up2, dn2, up3, dn3):
             cpy.wait_recv()
         for k in range(NZ):
             r = slice(k * ZB, (k + 1) * ZB)
-            zsend[it, k, :ZB] = mom[it, 0, r] + ring2[it, 0, r] + ring2[it, 1, r]
+            zsend[it, k] = mom[it, 0, r] + ring2[it, 0, r] + ring2[it, 1, r]
 
         for j in range(1, NZ):
             rdma(zsend.at[it, zo[j]], zrecv.at[it, j], s_z.at[it], r_z.at[it],
@@ -236,8 +263,10 @@
         shard = zsend[it, z]
         for j in range(1, NZ):
             shard += zrecv[it, j]
-
-        xall[it, x] = shard
+        arrived(statz.at[it, pl.ds(1, NZ - 1)], r_st.at[it, 1])
+
+        xall[it, x, :ZB] = shard
+        xall[it, x, ZB:] = jnp.sum(statz[it], axis=0)
         for j in range(1, NX):
             rdma(xall.at[it, x], xall.at[it, x], s_x.at[it], r_x.at[it], at(x_=xo[j])).start()
         arrived(xall.at[it, pl.ds(0, NX - 1)], r_x.at[it])
@@ -291,43 +320,39 @@
         squares_own = percol[:, 0:1]
         g = (
             squares_own * (facing_columns / facing_mass)
-            - 2.0 * (cross / facing_mass)
+            + cross * (-2.0 / facing_mass)
             + facing_norms / facing_mass
-        ) / marginal
+        ) * (1.0 / marginal)
         grad[...] = g
         centred = g - jnp.sum(g, axis=1, keepdims=True) * (1.0 / RANK)
         largest = jnp.max(jnp.abs(centred))
-
-        last = it == ITERS - 1
 
         @pl.when(last)
         def _():
             @pl.when(swapped)
             def _():
-                rdma(lf, fin.at[0], s_fin.at[0], r_fin.at[0], at(c_=vc, x_=xq)).start()
                 rdma(grad, fin.at[1], s_fin.at[1], r_fin.at[1], at(c_=vc, x_=xq)).start()
 
-        tile = (8, 128)
+        tile = (1, 128)
         mx[it, 0] = jnp.full(tile, largest)
-        for j in range(1, 8):
-            rdma(mx.at[it, 0], mx.at[it, j], s_mc.at[it], r_mc.at[it],
-                 at(c_=cx[j][0], x_=cx[j][1])).start()
-        for cpy in [cp, up1, dn1, up2, dn2, up3, dn3]:
+        for j in range(1, NY * NZ):
+            rdma(mx.at[it, 0], mx.at[it, j], s_my.at[it], r_my.at[it],
+                 at(y_=yz[j][0], z_=yz[j][1])).start()
+        for cpy in [cp, up1, dn1, up2, dn2, up3, dn3, pc] + gout:
             cpy.wait_send()
-        sent(stat.at[it, pl.ds(1, NY - 1)], s_st.at[it])
+        sent(stat.at[it, pl.ds(1, NY - 1)], s_st.at[it, 0])
+        sent(statz.at[it, pl.ds(1, NZ - 1)], s_st.at[it, 1])
         sent(zrecv.at[it, pl.ds(1, NZ - 1)], s_z.at[it])
-        arrived(mx.at[it, pl.ds(1, 7)], r_mc.at[it])
-        mx[it, 8] = jnp.max(mx[it, :8], axis=0)
-        for j in range(1, NY * NZ):
-            rdma(mx.at[it, 8], mx.at[it, 8 + j], s_my.at[it], r_my.at[it],
-                 at(y_=yz[j][0], z_=yz[j][1])).start()
         sent(xall.at[it, pl.ds(0, NX - 1)], s_x.at[it])
         sent(gath.at[it, y, pl.ds(0, (NZ - 1) * ZB)], s_gz.at[it])
-        for cpy in gout + [pc]:
-            cpy.wait_send()
-        sent(mx.at[it, pl.ds(1, 7)], s_mc.at[it])
-        arrived(mx.at[it, pl.ds(9, NY * NZ - 1)], r_my.at[it])
-        m = jnp.max(mx[it, 8:40], axis=0)
+        arrived(mx.at[it, pl.ds(1, NY * NZ - 1)], r_my.at[it])
+        mx[it, NY * NZ] = jnp.max(mx[it, : NY * NZ], axis=0)
+        for j in range(1, 8):
+            rdma(mx.at[it, NY * NZ], mx.at[it, NY * NZ + j], s_mc.at[it], r_mc.at[it],
+                 at(c_=cx[j][0], x_=cx[j][1])).start()
+        sent(mx.at[it, pl.ds(1, NY * NZ - 1)], s_my.at[it])
+        arrived(mx.at[it, pl.ds(NY * NZ + 1, 7)], r_mc.at[it])
+        m = jnp.max(mx[it, NY * NZ : NY * NZ + 8], axis=0)
         rate = STEP_SCALE / (m[0:1, 0:1] + 1e-6)
 
         @pl.when(jnp.logical_not(last))
@@ -353,7 +378,7 @@
             def _():
                 finish(lf[...], grad[...])
 
-        sent(mx.at[it, pl.ds(9, NY * NZ - 1)], s_my.at[it])
+        sent(mx.at[it, pl.ds(NY * NZ + 1, 7)], s_mc.at[it])
         return 0
 
     lax.fori_loop(0, ITERS, step, 0)
@@ -362,12 +387,9 @@
 
     @pl.when(swapped)
     def _():
-        lf_remote.wait_send()
         meta_own.wait_send()
-        for j in range(NY):
-            for r in range(2):
-                for h in range(2):
-                    piece(j, h, r).wait_send()
+        for j in range(2, NY):
+            each_piece(j, wait_send)
 
     @pl.when(jnp.logical_not(swapped))
     def _():
@@ -397,12 +419,13 @@
             vm(NY, 2 * ROWS, YB), vm(ROWS, 2 * HALF), vm(2, NY, 128, YB), vm(ROWS, RANK),
             vm(2, 8, ROWS), vm(8, ROWS), vm(ROWS, 8),
             vm(n, 2 * ROWS, RANK), vm(n, NY, YB, RANK), vm(n, 2, 128, RANK), vm(n, 2, YB, RANK),
-            vm(n, NY, 8, RANK), vm(n, NZ, ZS, RANK), vm(n, NZ, ZS, RANK), vm(n, NX, ZS, RANK),
+            vm(n, NY, 8, RANK), vm(n, NZ, 8, RANK), vm(n, NZ, ZB, RANK), vm(n, NZ, ZB, RANK),
+            vm(n, NX, ZS, RANK),
             vm(n, NY, YB, RANK), vm(2 * ROWS, RANK), vm(n, 2, ROWS, RANK),
-            vm(n, 40, 8, 128), vm(ROWS, RANK), vm(2, ROWS, RANK),
+            vm(n, 40, 1, 128), vm(ROWS, RANK), vm(2, ROWS, RANK),
             pltpu.SemaphoreType.DMA, dma(2, 2, NY), dma(2, NY), dma(2, NY),
             dma(2, NY), dma(NY, 2), pltpu.SemaphoreType.DMA, pltpu.SemaphoreType.DMA,
-            dma(2), dma(2), dma(n), dma(n), dma(n, 6), dma(n, 6), dma(n), dma(n),
+            dma(2), dma(2), dma(n), dma(n), dma(n, 6), dma(n, 6), dma(n, 2), dma(n, 2),
             dma(n), dma(n), dma(n), dma(n), dma(n), dma(n), dma(n, 6), dma(n, 6),
             dma(n), dma(n), dma(n), dma(n), dma(n), dma(n), dma(2), dma(2),
         ],

time: 148 us -> 139 us (0.939)
  Pallas kernels: 146 us -> 137 us
    pallas_call x1, Pallas kernels: 146 us -> 137 us  [body(): pl.pallas_call(kernel, out_shape=jax.ShapeDtypeStruct((ROWS, RANK), f32),...]
where the time goes in v4:
time: 139 us
  Pallas kernels  137 us (99%)
  other arithmetic  1.67 us (1%)
    pallas_call x1, Pallas kernels, body(): pl.pallas_call(kernel, out_shape=jax.ShapeDtypeStruct((ROWS, RANK), f32),...  137 us

profile of v4, /device:TPU:1, one launch (start us, length us, event | category | flops | bytes accessed | tf_op | source)
XLA Modules:
  0.0 139.0 jit_solution(14370287684211817023)
XLA Ops:
  0.0 137.3 %steps.1 = f32[256,256]{1,0:T(8,128)} custom-call(f32[256,2048]{1,0:T(8,128)} %points.1, f32[256,256]{1,0:T(8,128)} %lf_in.1, f32[1,256]{1,0:T(1,128)} %bitcast.1), custom_call_target="tpu_custom_call" | custom-call | tf_op jit(solution)/shard_map/steps/pallas_call | solution.py:412
  137.3 1.7 %broadcast_multiply_fusion = f32[256,256]{1,0:T(8,128)} fusion(f32[256,256]{1,0:T(8,128)} %steps.1), kind=kLoop, calls=%fused_computation | loop fusion | flops 65536 | bytes 524288 | tf_op jit(solution)/shard_map/mul | solution.py:437

commit v5 on v4

--- a/solution.py
+++ b/solution.py
@@ -63,8 +63,18 @@
     yo = [(y + j) % NY for j in range(NY)]
     zo = [(z + j) % NZ for j in range(NZ)]
     xo = [(x + j) % NX for j in range(NX)]
-    cx = [(c if i == 0 else other, xo[j]) for i in range(2) for j in range(NX)]
-    yz = [(yo[i], zo[j]) for i in range(NY) for j in range(NZ)]
+
+    def hops(k, n):
+        return min(k, n - k)
+
+    zf = sorted(range(1, NZ), key=lambda j: -hops(j, NZ))
+    xf = sorted(range(1, NX), key=lambda j: -hops(j, NX))
+    cx = [(i, j) for i in range(2) for j in range(NX)]
+    cx = sorted(cx, key=lambda k: -hops(k[1], NX) - 0.5 * k[0])
+    cx = [(c if i == 0 else other, xo[j]) for i, j in cx]
+    yz = [(i, j) for i in range(NY) for j in range(NZ)]
+    yz = sorted(yz, key=lambda k: -hops(k[0], NY) - hops(k[1], NZ))
+    yz = [(yo[i], zo[j]) for i, j in yz]
     own = pl.ds(pl.multiple_of(c * ROWS, ROWS), ROWS)
     oth = pl.ds(pl.multiple_of(other * ROWS, ROWS), ROWS)
     relays = x % 2 == 0
@@ -115,7 +125,7 @@
             half_local(b).start()
 
     barrier = pltpu.get_barrier_semaphore()
-    peers = [at(c_=a, x_=b) for a, b in cx[1:]] + [at(y_=a, z_=b) for a, b in yz[1:]]
+    peers = [at(y_=a, z_=b) for a, b in yz[:-1]] + [at(c_=a, x_=b) for a, b in cx[:-1]]
     for p in peers:
         pl.semaphore_signal(barrier, inc=1, device_id=p, device_id_type=pl.DeviceIdType.MESH)
 
@@ -247,7 +257,7 @@
 
         arrived(stat.at[it, pl.ds(1, NY - 1)], r_st.at[it, 0])
         statz[it, 0] = stat[it, 0] + stat[it, 1] + stat[it, 2] + stat[it, 3]
-        for j in range(1, NZ):
+        for j in zf:
             rdma(statz.at[it, 0], statz.at[it, j], s_st.at[it, 1], r_st.at[it, 1],
                  at(z_=zo[j])).start()
         for cpy in (up2, dn2, up3, dn3):
@@ -256,7 +266,7 @@
             r = slice(k * ZB, (k + 1) * ZB)
             zsend[it, k] = mom[it, 0, r] + ring2[it, 0, r] + ring2[it, 1, r]
 
-        for j in range(1, NZ):
+        for j in zf:
             rdma(zsend.at[it, zo[j]], zrecv.at[it, j], s_z.at[it], r_z.at[it],
                  at(z_=zo[j])).start()
         arrived(zrecv.at[it, pl.ds(1, NZ - 1)], r_z.at[it])
@@ -267,7 +277,7 @@
 
         xall[it, x, :ZB] = shard
         xall[it, x, ZB:] = jnp.sum(statz[it], axis=0)
-        for j in range(1, NX):
+        for j in xf:
             rdma(xall.at[it, x], xall.at[it, x], s_x.at[it], r_x.at[it], at(x_=xo[j])).start()
         arrived(xall.at[it, pl.ds(0, NX - 1)], r_x.at[it])
         source = xall[it, 0] + xall[it, 1] + xall[it, 2]
@@ -277,7 +287,7 @@
 
         zrows = pl.ds(pl.multiple_of(z * ZB, ZB), ZB)
         gath[it, y, zrows] = facing[:ZB]
-        for j in range(1, NZ):
+        for j in zf:
             rdma(gath.at[it, y, zrows], gath.at[it, y, zrows], s_gz.at[it], r_gz.at[it],
                  at(z_=zo[j])).start()
         source_mass = jnp.sum(source[ZB + 1 : ZB + 2])
@@ -337,7 +347,7 @@
         mx[it, 0] = jnp.full(tile, largest)
         for j in range(1, NY * NZ):
             rdma(mx.at[it, 0], mx.at[it, j], s_my.at[it], r_my.at[it],
-                 at(y_=yz[j][0], z_=yz[j][1])).start()
+                 at(y_=yz[j - 1][0], z_=yz[j - 1][1])).start()
         for cpy in [cp, up1, dn1, up2, dn2, up3, dn3, pc] + gout:
             cpy.wait_send()
         sent(stat.at[it, pl.ds(1, NY - 1)], s_st.at[it, 0])
@@ -349,7 +359,7 @@
         mx[it, NY * NZ] = jnp.max(mx[it, : NY * NZ], axis=0)
         for j in range(1, 8):
             rdma(mx.at[it, NY * NZ], mx.at[it, NY * NZ + j], s_mc.at[it], r_mc.at[it],
-                 at(c_=cx[j][0], x_=cx[j][1])).start()
+                 at(c_=cx[j - 1][0], x_=cx[j - 1][1])).start()
         sent(mx.at[it, pl.ds(1, NY * NZ - 1)], s_my.at[it])
         arrived(mx.at[it, pl.ds(NY * NZ + 1, 7)], r_mc.at[it])
         m = jnp.max(mx[it, NY * NZ : NY * NZ + 8], axis=0)
@@ -411,7 +421,7 @@
     n = ITERS
     share = pl.pallas_call(
         kernel,
-        out_shape=jax.ShapeDtypeStruct((ROWS, RANK), f32),
+        out_shape=pltpu.VMEM((ROWS, RANK), f32),
         in_specs=[pl.BlockSpec(memory_space=pltpu.HBM)] * 2
         + [pl.BlockSpec(memory_space=pltpu.VMEM)],
         out_specs=pl.BlockSpec(memory_space=pltpu.VMEM),

time: 139 us -> 135 us (0.971)
  Pallas kernels: 137 us -> 134 us
    pallas_call x1, Pallas kernels: 137 us -> 134 us  [body(): pl.pallas_call(kernel, out_shape=pltpu.VMEM((ROWS, RANK), f32), in_specs=...]
where the time goes in v5:
time: 135 us
  Pallas kernels  134 us (99%)
    pallas_call x1, Pallas kernels, body(): pl.pallas_call(kernel, out_shape=pltpu.VMEM((ROWS, RANK), f32), in_specs=...  134 us

profile of v5, /device:TPU:1, one launch (start us, length us, event | category | flops | bytes accessed | tf_op | source)
XLA Modules:
  0.0 134.9 jit_solution(18414946082195849958)
XLA Ops:
  0.0 134.2 %steps.1 = f32[256,256]{1,0:T(8,128)S(1)} custom-call(f32[256,2048]{1,0:T(8,128)} %points.1, f32[256,256]{1,0:T(8,128)} %lf_in.1, f32[1,256]{1,0:T(1,128)} %bitcast.1), custom_call_target="tpu_custom_call" | custom-call | tf_op jit(solution)/shard_map/steps/pallas_call | solution.py:422
  134.2 0.7 broadcast_multiply_fusion

commit v6 on v5

--- a/solution.py
+++ b/solution.py
@@ -18,6 +18,8 @@
 YB = HALF // NY
 ZB = YB // NZ
 ZS = ZB + 8
+ZA, ZY = ZB - 8, 8
+YA = NZ * ZA
 HIGHEST = lax.Precision.HIGHEST
 
 
@@ -38,7 +40,7 @@
     pts, pv, relay, lf, meta, meta_out, percol, scaled, mom, ring1, ring2, stat, statz, zsend, zrecv, xall, gath, acc, part,
     mx, grad, fin,
     r_pv, s_rel, r_rel, s_fwd, s_pts, r_pts, s_lf, r_lf, s_meta, r_meta, s_sc, r_sc, s_r, r_r, s_st, r_st,
-    s_z, r_z, s_x, r_x, s_gz, r_gz, s_gy, r_gy, s_pt, r_pt, s_mc, r_mc, s_my, r_my,
+    s_z, r_z, s_x, r_x, s_gz, r_gz, s_gb, r_gb, s_gy, r_gy, s_pt, r_pt, s_mc, r_mc, s_my, r_my,
     s_fin, r_fin,
 ):
     xl, c, y, xh, z = (lax.axis_index(a) for a in AXES)
@@ -262,13 +264,17 @@
                  at(z_=zo[j])).start()
         for cpy in (up2, dn2, up3, dn3):
             cpy.wait_recv()
-        for k in range(NZ):
-            r = slice(k * ZB, (k + 1) * ZB)
-            zsend[it, k] = mom[it, 0, r] + ring2[it, 0, r] + ring2[it, 1, r]
+
+        def fill(k):
+            for dst, n, first in ((0, ZA, k * ZA), (ZA, ZY, YA + k * ZY)):
+                r = pl.ds(pl.multiple_of(first, 8), n)
+                zsend[it, k, dst : dst + n] = mom[it, 0, r] + ring2[it, 0, r] + ring2[it, 1, r]
 
         for j in zf:
+            fill(zo[j])
             rdma(zsend.at[it, zo[j]], zrecv.at[it, j], s_z.at[it], r_z.at[it],
                  at(z_=zo[j])).start()
+        fill(z)
         arrived(zrecv.at[it, pl.ds(1, NZ - 1)], r_z.at[it])
         shard = zsend[it, z]
         for j in range(1, NZ):
@@ -285,8 +291,13 @@
         is_target = x == 3
         facing = jnp.where(is_target, source, target)
 
-        zrows = pl.ds(pl.multiple_of(z * ZB, ZB), ZB)
-        gath[it, y, zrows] = facing[:ZB]
+        zrows = pl.ds(pl.multiple_of(z * ZA, 8), ZA)
+        yrows = pl.ds(pl.multiple_of(YA + z * ZY, 8), ZY)
+        gath[it, y, zrows] = facing[:ZA]
+        gath[it, y, yrows] = facing[ZA:ZB]
+        for j in (2, 1, 3):
+            rdma(gath.at[it, y, yrows], gath.at[it, y, yrows], s_gb.at[it, 0], r_gb.at[it, 0],
+                 at(y_=yo[j])).start()
         for j in zf:
             rdma(gath.at[it, y, zrows], gath.at[it, y, zrows], s_gz.at[it], r_gz.at[it],
                  at(z_=zo[j])).start()
@@ -295,29 +306,35 @@
         facing_mass = jnp.where(is_target, source_mass, target_mass)
         marginal = 0.5 * (source[ZB + 1 : ZB + 2] / source_mass
                           + target[ZB + 1 : ZB + 2] / target_mass)
-        arrived(gath.at[it, y, pl.ds(0, (NZ - 1) * ZB)], r_gz.at[it])
+        arrived(gath.at[it, pl.ds(0, NY - 1), yrows], r_gb.at[it, 0])
+        every = gath.at[it, pl.ds(0, NY), yrows]
+        for j in zf:
+            rdma(every, every, s_gb.at[it, 1], r_gb.at[it, 1], at(z_=zo[j])).start()
+        arrived(gath.at[it, y, pl.ds(0, (NZ - 1) * ZA)], r_gz.at[it])
+        glo, ghi = pl.ds(0, YA // 2), pl.ds(YA // 2, YA // 2)
 
         def block(b, rows, n, dev):
             ref = gath.at[it, b, rows]
             return rdma(ref, ref, s_gy.at[it, n], r_gy.at[it, n], dev)
 
-        gout = [block(y, lo, 0, up), block(y, hi, 1, dn), block(y, hi, 2, up),
-                block(y, lo, 3, dn)]
+        gout = [block(y, glo, 0, up), block(y, ghi, 1, dn), block(y, ghi, 2, up),
+                block(y, glo, 3, dn)]
         for cpy in gout:
             cpy.start()
+        block(yo[3], glo, 0, up).wait_recv()
+        gout += [block(yo[3], glo, 4, up)]
+        gout[4].start()
+        block(yo[1], ghi, 1, dn).wait_recv()
+        gout += [block(yo[1], ghi, 5, dn)]
+        gout[5].start()
+        arrived(gath.at[it, 0, pl.ds(0, (NZ - 1) * NY * ZY)], r_gb.at[it, 1])
         acc[...] = dot1(pts[y], gath[it, y])
-        block(yo[3], lo, 0, up).wait_recv()
-        gout += [block(yo[3], lo, 4, up)]
-        gout[4].start()
-        block(yo[1], hi, 1, dn).wait_recv()
-        gout += [block(yo[1], hi, 5, dn)]
-        gout[5].start()
-        block(yo[3], hi, 2, up).wait_recv()
+        block(yo[3], ghi, 2, up).wait_recv()
         acc[...] += dot1(pts[yo[3]], gath[it, yo[3]])
-        block(yo[1], lo, 3, dn).wait_recv()
+        block(yo[1], glo, 3, dn).wait_recv()
         acc[...] += dot1(pts[yo[1]], gath[it, yo[1]])
-        block(yo[2], lo, 4, up).wait_recv()
-        block(yo[2], hi, 5, dn).wait_recv()
+        block(yo[2], glo, 4, up).wait_recv()
+        block(yo[2], ghi, 5, dn).wait_recv()
         part[it, 0] = acc[oth] + dot1(pts[yo[2], oth], gath[it, yo[2]])
         pc = rdma(part.at[it, 0], part.at[it, 1], s_pt.at[it], r_pt.at[it], at(c_=other))
         pc.start()
@@ -354,7 +371,9 @@
         sent(statz.at[it, pl.ds(1, NZ - 1)], s_st.at[it, 1])
         sent(zrecv.at[it, pl.ds(1, NZ - 1)], s_z.at[it])
         sent(xall.at[it, pl.ds(0, NX - 1)], s_x.at[it])
-        sent(gath.at[it, y, pl.ds(0, (NZ - 1) * ZB)], s_gz.at[it])
+        sent(gath.at[it, y, pl.ds(0, (NZ - 1) * ZA)], s_gz.at[it])
+        sent(gath.at[it, pl.ds(0, NY - 1), yrows], s_gb.at[it, 0])
+        sent(gath.at[it, 0, pl.ds(0, (NZ - 1) * NY * ZY)], s_gb.at[it, 1])
         arrived(mx.at[it, pl.ds(1, NY * NZ - 1)], r_my.at[it])
         mx[it, NY * NZ] = jnp.max(mx[it, : NY * NZ], axis=0)
         for j in range(1, 8):
@@ -436,7 +455,7 @@
             pltpu.SemaphoreType.DMA, dma(2, 2, NY), dma(2, NY), dma(2, NY),
             dma(2, NY), dma(NY, 2), pltpu.SemaphoreType.DMA, pltpu.SemaphoreType.DMA,
             dma(2), dma(2), dma(n), dma(n), dma(n, 6), dma(n, 6), dma(n, 2), dma(n, 2),
-            dma(n), dma(n), dma(n), dma(n), dma(n), dma(n), dma(n, 6), dma(n, 6),
+            dma(n), dma(n), dma(n), dma(n), dma(n), dma(n), dma(n, 2), dma(n, 2), dma(n, 6), dma(n, 6),
             dma(n), dma(n), dma(n), dma(n), dma(n), dma(n), dma(2), dma(2),
         ],
         compiler_params=pltpu.CompilerParams(

time: 135 us -> 133 us (0.985)
  Pallas kernels: 134 us -> 132 us
    pallas_call x1, Pallas kernels: 134 us -> 132 us  [body(): pl.pallas_call(kernel, out_shape=pltpu.VMEM((ROWS, RANK), f32), in_specs=...]
where the time goes in v6:
time: 133 us
  Pallas kernels  132 us (99%)
    pallas_call x1, Pallas kernels, body(): pl.pallas_call(kernel, out_shape=pltpu.VMEM((ROWS, RANK), f32), in_specs=...  132 us

profile of v6, /device:TPU:1, one launch (start us, length us, event | category | flops | bytes accessed | tf_op | source)
XLA Modules:
  0.0 132.9 jit_solution(15280099943718558993)
XLA Ops:
  0.0 132.2 %steps.1 = f32[256,256]{1,0:T(8,128)S(1)} custom-call(f32[256,2048]{1,0:T(8,128)} %points.1, f32[256,256]{1,0:T(8,128)} %lf_in.1, f32[1,256]{1,0:T(1,128)} %bitcast.1), custom_call_target="tpu_custom_call" | custom-call | tf_op jit(solution)/shard_map/steps/pallas_call | solution.py:441
  132.2 0.7 broadcast_multiply_fusion

commit v7 on v6

--- a/solution.py
+++ b/solution.py
@@ -71,12 +71,12 @@
 
     zf = sorted(range(1, NZ), key=lambda j: -hops(j, NZ))
     xf = sorted(range(1, NX), key=lambda j: -hops(j, NX))
-    cx = [(i, j) for i in range(2) for j in range(NX)]
-    cx = sorted(cx, key=lambda k: -hops(k[1], NX) - 0.5 * k[0])
-    cx = [(c if i == 0 else other, xo[j]) for i, j in cx]
-    yz = [(i, j) for i in range(NY) for j in range(NZ)]
-    yz = sorted(yz, key=lambda k: -hops(k[0], NY) - hops(k[1], NZ))
-    yz = [(yo[i], zo[j]) for i, j in yz]
+    cz = [(i, j) for i in range(2) for j in range(NZ)]
+    cz = sorted(cz, key=lambda k: -hops(k[1], NZ) - 0.5 * k[0])
+    cz = [(c if i == 0 else other, zo[j]) for i, j in cz]
+    xy = [(i, j) for i in range(NX) for j in range(NY)]
+    xy = sorted(xy, key=lambda k: -hops(k[0], NX) - hops(k[1], NY))
+    xy = [(xo[i], yo[j]) for i, j in xy]
     own = pl.ds(pl.multiple_of(c * ROWS, ROWS), ROWS)
     oth = pl.ds(pl.multiple_of(other * ROWS, ROWS), ROWS)
     relays = x % 2 == 0
@@ -127,7 +127,8 @@
             half_local(b).start()
 
     barrier = pltpu.get_barrier_semaphore()
-    peers = [at(y_=a, z_=b) for a, b in yz[:-1]] + [at(c_=a, x_=b) for a, b in cx[:-1]]
+    peers = [at(c_=a, z_=b) for a, b in cz[:-1]] + [at(x_=a, y_=b) for a, b in xy[:-1]]
+    peers += [at(c_=other, x_=b) for b in xo[1:]]
     for p in peers:
         pl.semaphore_signal(barrier, inc=1, device_id=p, device_id_type=pl.DeviceIdType.MESH)
 
@@ -191,12 +192,14 @@
             rdma(dst, dst, s_pts.at[0, b], r_pts.at[b, v], at(c_=other)).wait_recv()
 
     def step(it, _):
-        v = lf[...]
-        e = jnp.exp(v - jnp.max(v, axis=1, keepdims=True))
-        mass_own = percol[:, 2:3]
-        scaled[it, own] = e / jnp.sum(e, axis=1, keepdims=True) * mass_own
-        cp = rdma(scaled.at[it, own], scaled.at[it, own], s_sc.at[it], r_sc.at[it], at(c_=other))
-        cp.start()
+        for k in range(2):
+            half = slice(k * 128, (k + 1) * 128)
+            v = lf[half]
+            e = jnp.exp(v - jnp.max(v, axis=1, keepdims=True))
+            rows = pl.ds(pl.multiple_of(c * ROWS + k * 128, 128), 128)
+            scaled[it, rows] = e / jnp.sum(e, axis=1, keepdims=True) * percol[half, 2:3]
+            rdma(scaled.at[it, rows], scaled.at[it, rows], s_sc.at[it], r_sc.at[it],
+                 at(c_=other)).start()
         last = it == ITERS - 1
 
         @pl.when(last)
@@ -362,11 +365,12 @@
 
         tile = (1, 128)
         mx[it, 0] = jnp.full(tile, largest)
-        for j in range(1, NY * NZ):
-            rdma(mx.at[it, 0], mx.at[it, j], s_my.at[it], r_my.at[it],
-                 at(y_=yz[j - 1][0], z_=yz[j - 1][1])).start()
-        for cpy in [cp, up1, dn1, up2, dn2, up3, dn3, pc] + gout:
+        for j in range(1, 16):
+            rdma(mx.at[it, 0], mx.at[it, j], s_mc.at[it], r_mc.at[it],
+                 at(c_=cz[j - 1][0], z_=cz[j - 1][1])).start()
+        for cpy in [up1, dn1, up2, dn2, up3, dn3, pc] + gout:
             cpy.wait_send()
+        sent(scaled.at[it, own], s_sc.at[it])
         sent(stat.at[it, pl.ds(1, NY - 1)], s_st.at[it, 0])
         sent(statz.at[it, pl.ds(1, NZ - 1)], s_st.at[it, 1])
         sent(zrecv.at[it, pl.ds(1, NZ - 1)], s_z.at[it])
@@ -374,14 +378,14 @@
         sent(gath.at[it, y, pl.ds(0, (NZ - 1) * ZA)], s_gz.at[it])
         sent(gath.at[it, pl.ds(0, NY - 1), yrows], s_gb.at[it, 0])
         sent(gath.at[it, 0, pl.ds(0, (NZ - 1) * NY * ZY)], s_gb.at[it, 1])
-        arrived(mx.at[it, pl.ds(1, NY * NZ - 1)], r_my.at[it])
-        mx[it, NY * NZ] = jnp.max(mx[it, : NY * NZ], axis=0)
-        for j in range(1, 8):
-            rdma(mx.at[it, NY * NZ], mx.at[it, NY * NZ + j], s_mc.at[it], r_mc.at[it],
-                 at(c_=cx[j - 1][0], x_=cx[j - 1][1])).start()
-        sent(mx.at[it, pl.ds(1, NY * NZ - 1)], s_my.at[it])
-        arrived(mx.at[it, pl.ds(NY * NZ + 1, 7)], r_mc.at[it])
-        m = jnp.max(mx[it, NY * NZ : NY * NZ + 8], axis=0)
+        arrived(mx.at[it, pl.ds(1, 15)], r_mc.at[it])
+        mx[it, 16] = jnp.max(mx[it, :16], axis=0)
+        for j in range(1, 16):
+            rdma(mx.at[it, 16], mx.at[it, 16 + j], s_my.at[it], r_my.at[it],
+                 at(x_=xy[j - 1][0], y_=xy[j - 1][1])).start()
+        sent(mx.at[it, pl.ds(1, 15)], s_mc.at[it])
+        arrived(mx.at[it, pl.ds(17, 15)], r_my.at[it])
+        m = jnp.max(mx[it, 16:32], axis=0)
         rate = STEP_SCALE / (m[0:1, 0:1] + 1e-6)
 
         @pl.when(jnp.logical_not(last))
@@ -407,7 +411,7 @@
             def _():
                 finish(lf[...], grad[...])
 
-        sent(mx.at[it, pl.ds(NY * NZ + 1, 7)], s_mc.at[it])
+        sent(mx.at[it, pl.ds(17, 15)], s_my.at[it])
         return 0
 
     lax.fori_loop(0, ITERS, step, 0)
@@ -451,7 +455,7 @@
             vm(n, NY, 8, RANK), vm(n, NZ, 8, RANK), vm(n, NZ, ZB, RANK), vm(n, NZ, ZB, RANK),
             vm(n, NX, ZS, RANK),
             vm(n, NY, YB, RANK), vm(2 * ROWS, RANK), vm(n, 2, ROWS, RANK),
-            vm(n, 40, 1, 128), vm(ROWS, RANK), vm(2, ROWS, RANK),
+            vm(n, 32, 1, 128), vm(ROWS, RANK), vm(2, ROWS, RANK),
             pltpu.SemaphoreType.DMA, dma(2, 2, NY), dma(2, NY), dma(2, NY),
             dma(2, NY), dma(NY, 2), pltpu.SemaphoreType.DMA, pltpu.SemaphoreType.DMA,
             dma(2), dma(2), dma(n), dma(n), dma(n, 6), dma(n, 6), dma(n, 2), dma(n, 2),

time: 133 us -> 131 us (0.985)
    pallas_call x1, Pallas kernels: 132 us -> 131 us  [body(): pl.pallas_call(kernel, out_shape=pltpu.VMEM((ROWS, RANK), f32), in_specs=...]
where the time goes in v7:
time: 131 us
  Pallas kernels  131 us (100%)
    pallas_call x1, Pallas kernels, body(): pl.pallas_call(kernel, out_shape=pltpu.VMEM((ROWS, RANK), f32), in_specs=...  131 us

profile of v7, /device:TPU:1, one launch (start us, length us, event | category | flops | bytes accessed | tf_op | source)
XLA Modules:
  0.0 131.3 jit_solution(8133899772361255501)
XLA Ops:
  0.0 130.6 %steps.1 = f32[256,256]{1,0:T(8,128)S(1)} custom-call(f32[256,2048]{1,0:T(8,128)} %points.1, f32[256,256]{1,0:T(8,128)} %lf_in.1, f32[1,256]{1,0:T(1,128)} %bitcast.1), custom_call_target="tpu_custom_call" | custom-call | tf_op jit(solution)/shard_map/steps/pallas_call | solution.py:445
  130.6 0.7 broadcast_multiply_fusion

commit v8 on v7

--- a/solution.py
+++ b/solution.py
@@ -208,15 +208,19 @@
             def _():
                 rdma(lf, fin.at[0], s_fin.at[0], r_fin.at[0], at(c_=vc, x_=xq)).start()
 
+        def pass_on(j):
+            @pl.when((it == 0) & relays)
+            def _():
+                for r in range(2):
+                    piece(j, c, r).wait_recv()
+                    forward(j, r).start()
+
         def ready(j):
+            if j < 3:
+                pass_on(j)
+
             @pl.when(it == 0)
             def _():
-                @pl.when(relays)
-                def _():
-                    for r in range(2):
-                        piece(j, c, r).wait_recv()
-                        forward(j, r).start()
-
                 if j < 2:
                     @pl.when(swapped)
                     def _():
@@ -247,6 +251,7 @@
         up2 = ring(1, hi, ring2.at[it, 0, hi], 2, up)
         mom[it, 3] = moment(2)
         dn2 = ring(3, lo, ring2.at[it, 1, lo], 3, dn)
+        pass_on(3)
         stat[it, 0] = dot1(meta[0], scaled[it, :ROWS]) + dot1(meta[1], scaled[it, ROWS:])
         for j in range(1, NY):
             rdma(stat.at[it, 0], stat.at[it, j], s_st.at[it, 0], r_st.at[it, 0],

time: 131 us -> 131 us (level)
  no operation moved by 1% of the time
where the time goes in v8:
time: 131 us
  Pallas kernels  131 us (100%)
    pallas_call x1, Pallas kernels, body(): pl.pallas_call(kernel, out_shape=pltpu.VMEM((ROWS, RANK), f32), in_specs=...  131 us

profile of v8, /device:TPU:1, one launch (start us, length us, event | category | flops | bytes accessed | tf_op | source)
XLA Modules:
  0.0 131.4 jit_solution(1563220932031580476)
XLA Ops:
  0.0 130.6 %steps.1 = f32[256,256]{1,0:T(8,128)S(1)} custom-call(f32[256,2048]{1,0:T(8,128)} %points.1, f32[256,256]{1,0:T(8,128)} %lf_in.1, f32[1,256]{1,0:T(1,128)} %bitcast.1), custom_call_target="tpu_custom_call" | custom-call | tf_op jit(solution)/shard_map/steps/pallas_call | solution.py:450
  130.6 0.7 broadcast_multiply_fusion

commit v9 on v8

--- a/solution.py
+++ b/solution.py
@@ -175,6 +175,7 @@
         each_piece(0, start)
         lf_remote.wait_send()
         each_piece(1, start)
+        each_piece(2, start)
 
     @pl.when(jnp.logical_not(swapped))
     def _():
@@ -221,11 +222,11 @@
 
             @pl.when(it == 0)
             def _():
-                if j < 2:
+                if j == 0:
                     @pl.when(swapped)
                     def _():
                         each_piece(j, wait_send)
-                        each_piece(j + 2, start)
+                        each_piece(j + 3, start)
 
                 wait_points(order[j])
 
@@ -426,7 +427,7 @@
     @pl.when(swapped)
     def _():
         meta_own.wait_send()
-        for j in range(2, NY):
+        for j in range(1, NY):
             each_piece(j, wait_send)
 
     @pl.when(jnp.logical_not(swapped))

time: 131 us -> 131 us (level)
  no operation moved by 1% of the time
where the time goes in v9:
time: 131 us
  Pallas kernels  131 us (100%)
    pallas_call x1, Pallas kernels, body(): pl.pallas_call(kernel, out_shape=pltpu.VMEM((ROWS, RANK), f32), in_specs=...  131 us

profile of v9, /device:TPU:1, one launch (start us, length us, event | category | flops | bytes accessed | tf_op | source)
XLA Modules:
  0.0 131.4 jit_solution(9382154306824696030)
XLA Ops:
  0.0 130.6 %steps.1 = f32[256,256]{1,0:T(8,128)S(1)} custom-call(f32[256,2048]{1,0:T(8,128)} %points.1, f32[256,256]{1,0:T(8,128)} %lf_in.1, f32[1,256]{1,0:T(1,128)} %bitcast.1), custom_call_target="tpu_custom_call" | custom-call | tf_op jit(solution)/shard_map/steps/pallas_call | solution.py:451
  130.6 0.7 broadcast_multiply_fusion
